TPU v7x, 32 devices: a whole 2x2x4 slice. The times are simulated.
32 devices in a mesh: clips: 2 (over x), ulysses: 4 (over y, core), tm: 4 (over z).
Axes of the slice: x: 2, y: 2, z: 4, core: 2. Of those that a mesh axis runs over, the one named last changes fastest.
Arguments:
- queries: bfloat16 [4096, 3072], P(('clips', 'tm', 'ulysses')), parts along dimension 0, may hold values from -90 to 90
- key_vectors: bfloat16 [4096, 3072], P(('clips', 'tm', 'ulysses')), parts along dimension 0, may hold values from -5 to 5
- value_vectors: bfloat16 [4096, 3072], P(('clips', 'tm', 'ulysses')), parts along dimension 0, may hold values from -6 to 6
- grad_out: bfloat16 [4096, 3072], P(('clips', 'tm', 'ulysses')), parts along dimension 0, may hold values from -6 to 6
- key_tiles: int32 [64, 3], P('clips'), parts along dimension 0, may hold values from 0 to 31, as said below
- tile_counts: int32 [64], P('clips'), parts along dimension 0, may hold values from 2 to 3, as said below
Outputs:
- attended: bfloat16 [4096, 3072], P(('clips', 'tm', 'ulysses')), parts along dimension 0
- grad_queries: bfloat16 [4096, 3072], P(('clips', 'tm', 'ulysses')), parts along dimension 0
- grad_keys: bfloat16 [4096, 3072], P(('clips', 'tm', 'ulysses')), parts along dimension 0
- grad_values: bfloat16 [4096, 3072], P(('clips', 'tm', 'ulysses')), parts along dimension 0
There are 2 independent parts, one for each index of `clips`. A program takes and returns all parts, laid end to end along the dimension named above; each array names one. Nothing has to cross between parts.
Inputs may be any that keep to these rules, and one draw needn't show every extreme that they name: `key_tiles`: row i holds distinct tiles of the frame of query tile i and of the frames just before and after it; entry 0 is tile i itself, then one tile of the frame before and one of the frame after where those frames exist, then the rest in no fixed order; entries from position tile_counts[i] on repeat entry 0. The query tiles of one frame together list exactly 1 tiles of the frame before it and exactly 1 of the frame after it, where those frames exist. `tile_counts`: the first 1 query tiles of every frame have count 3.
All inputs are finite; a program needn't handle non-finite values.
Results may differ from a plain program's by a relative error of at most 0.022.
Values may be sent and summed in bfloat16 or wider, within the bound.
No kernel may reach another device: no remote copies, remote signals or barrier semaphores. Data moves between devices by JAX's collectives and lax.ppermute only.
A program may use at most 192 MiB of HBM per device.

v0:
```python
import functools

import jax
import jax.numpy as jnp
from jax import lax
from jax.experimental import pallas as pl
from jax.experimental.pallas import tpu as pltpu
from jax.sharding import PartitionSpec as P

HEAD_DIM = 64
TILE = 64
FRAMES_SLAB = 2
PAIR = 2 * HEAD_DIM
BLOCK = 32
NEG = -1e30
VMEM_LIMIT = 24 * 1024 * 1024


class Plan:
    def __init__(self, rows, width, list_width):
        self.rows, self.width, self.list_width = rows, width, list_width
        self.slab = lax.axis_size("ulysses")
        self.slabs = lax.axis_size("tm")
        self.members = self.slab // FRAMES_SLAB
        self.frames = self.slabs * FRAMES_SLAB
        self.cols = width // self.members
        self.pairs = self.cols // PAIR
        self.device_tiles = rows // TILE
        self.frame_tiles = self.members * self.device_tiles
        self.remote = max(1, self.frame_tiles // 8)
        self.ext_tiles = self.frame_tiles + 2 * self.remote
        chunks = 2 if self.pairs % 2 == 0 else 1
        self.chunk_pairs = [self.pairs // chunks] * chunks
        self.span = 2 if self.chunk_pairs[0] % 2 == 0 else 1
        self.lanes = self.span * PAIR
        self.blocks = [count // self.span for count in self.chunk_pairs]
        self.unrolled = self.blocks[0] if self.frame_tiles <= 4 else 1
        self.whole_pieces = self.members == 2
        self.chunk_starts = [sum(self.chunk_pairs[:i]) for i in range(chunks)]

    def device(self, frame, member):
        place = frame % FRAMES_SLAB * self.members + member
        return place * self.slabs + frame // FRAMES_SLAB

    def member_perm(self, shift):
        return [
            (self.device(f, c), self.device(f, (c + shift) % self.members))
            for f in range(self.frames)
            for c in range(self.members)
        ]

    def frame_perm(self, far):
        pairs = [(f, partner(f, far)) for f in range(self.frames)]
        return [
            (self.device(f, c), self.device(other, c))
            for f, other in pairs
            if 0 <= other < self.frames
            for c in range(self.members)
        ]


def partner(frame, far):
    odd = frame % 2
    return frame - 1 + 2 * odd if far else frame + 1 - 2 * odd


def position(plan):
    place = lax.axis_index("ulysses")
    return lax.axis_index("tm") * FRAMES_SLAB + place // plan.members, place % plan.members


def piece_start(plan, me, offset):
    return pl.multiple_of(me * plan.cols + offset, PAIR) if plan.whole_pieces else offset


def listed(plan, lists_ref, counts_ref, reader, source):
    tiles = plan.frame_tiles
    row_start = jnp.clip(reader, 0, plan.frames - 1) * tiles
    base = source * tiles
    if plan.remote == 1:
        best = jnp.int32(0)
        for t in range(tiles):
            for j in range(plan.list_width):
                local = lists_ref[j, row_start + t] - base
                inside = (local >= 0) & (local < tiles) & (j < counts_ref[row_start + t])
                best = jnp.where(inside, local, best)
        return [best]

    def candidate(c, state):
        def row(t, found):
            for j in range(plan.list_width):
                hit = (lists_ref[j, row_start + t] == base + c) & (j < counts_ref[row_start + t])
                found = jnp.where(hit, 1, found)
            return found

        found = lax.fori_loop(0, tiles, row, jnp.int32(0))
        seen, picks = state
        picks = tuple(jnp.where((found == 1) & (seen == i), c, pick) for i, pick in enumerate(picks))
        return seen + found, picks

    start = (jnp.int32(0), tuple(jnp.int32(0) for _ in range(plan.remote)))
    return list(lax.fori_loop(0, tiles, candidate, start)[1])


def split_kernel(plan, *refs):
    count = (len(refs) - 1) // plan.members
    sources, outs, sem = refs[:count], refs[count:-1], refs[-1]
    _, me = position(plan)
    copies = []
    for r in range(1, plan.members):
        columns = pl.ds(pl.multiple_of((me + r) % plan.members * plan.cols, PAIR), plan.cols)
        for a, source in enumerate(sources):
            for row in range(0, plan.rows, BLOCK):
                rows = pl.ds(row, BLOCK)
                slot = len(copies)
                copies.append(
                    pltpu.make_async_copy(source.at[rows, columns], outs[(r - 1) * count + a].at[rows, :], sem.at[slot])
                )
    for copy in copies:
        copy.start()
    for copy in copies:
        copy.wait()


def slice_kernel(plan, after, *refs):
    refs = refs[after:]
    count = len(refs) // plan.members
    _, me = position(plan)
    for r in range(1, plan.members):
        columns = pl.ds(pl.multiple_of((me + r) % plan.members * plan.cols, PAIR), plan.cols)
        for a in range(count):
            refs[r * count + a][...] = refs[a][:, columns]


def pick_kernel(plan, g, lists_ref, counts_ref, *refs):
    members = plan.members
    own = refs[:2]
    pieces = refs[2 : 2 * members]
    outs = refs[-2:]
    frame, me = position(plan)
    cols = plan.chunk_pairs[g] * PAIR
    offset = plan.chunk_starts[g] * PAIR
    for far in range(2):
        picks = listed(plan, lists_ref, counts_ref, partner(frame, far), frame)
        for j, pick in enumerate(picks):
            owner = pick // plan.device_tiles
            row = pl.multiple_of(pick % plan.device_tiles * TILE, TILE)
            place = (me + members - owner) % members

            @pl.when(place == 0)
            def _():
                start = pl.multiple_of(me * plan.cols + offset, PAIR)
                for a in range(2):
                    outs[far][a, j] = own[a][pl.ds(row, TILE), pl.ds(start, cols)]

            for r in range(1, members):

                @pl.when(place == r)
                def _():
                    for a in range(2):
                        piece = pieces[(r - 1) * 2 + a]
                        outs[far][a, j] = piece[pl.ds(row, TILE), pl.ds(piece_start(plan, me, offset), cols)]


def attend_kernel(plan, g, lists_ref, counts_ref, *refs):
    members, tiles, remote, width = plan.members, plan.frame_tiles, plan.remote, plan.list_width
    per = plan.device_tiles
    others = members - 1
    own = refs[:4]
    key_value = refs[4 : 4 + 2 * others]
    query_grad = refs[4 + 2 * others : 4 + 4 * others]
    borders = refs[4 + 4 * others : 6 + 4 * others]
    rest = refs[6 + 4 * others :]
    earlier, rest = rest[: g * members], rest[g * members :]
    outs, parts = rest[:members], rest[members : members + 2]
    k_s, v_s, dk_s, dv_s, slots = rest[members + 2 :]
    last = g == len(plan.chunk_pairs) - 1
    for c in range(g if last else 0):
        done = pl.ds(plan.chunk_starts[c] * PAIR, plan.chunk_pairs[c] * PAIR)
        for r in range(members):
            outs[r][:, :, done] = earlier[c * members + r][...]
    frame, me = position(plan)
    partners = [partner(frame, far) for far in range(2)]
    known = [listed(plan, lists_ref, counts_ref, frame, other) for other in partners]
    live = []
    for t in range(tiles):
        row = frame * tiles + (me + members - t // per) % members * per + t % per
        live.append(counts_ref[row])
        for j in range(width):
            tile = lists_ref[j, row]
            local = tile - frame * tiles
            slot = (me + members - local // per) % members * per + local % per
            for far in range(2):
                local = tile - partners[far] * tiles
                rank = jnp.int32(0)
                for i in range(1, remote):
                    rank = jnp.where(local == known[far][i], i, rank)
                inside = (local >= 0) & (local < tiles)
                slot = jnp.where(inside, tiles + far * remote + rank, slot)
            slots[t, j] = slot

    lanes, heads = plan.lanes, plan.lanes // HEAD_DIM
    head_of = lax.broadcasted_iota(jnp.int32, (TILE, lanes), 1) // HEAD_DIM
    first = lax.broadcasted_iota(jnp.int32, (TILE, PAIR), 1) < HEAD_DIM
    scale = HEAD_DIM ** (-0.5)
    natural = (((1,), (0,)), ((), ()))
    inner = (((1,), (1,)), ((), ()))
    outer = (((0,), (0,)), ((), ()))

    def dot(left, right, dims):
        return lax.dot_general(left, right, dims, preferred_element_type=jnp.float32)

    def apart(rows):
        zero = jnp.zeros_like(rows)
        return jnp.concatenate([jnp.where(head_of == h, rows, zero) for h in range(heads)], axis=0)

    def together(terms, rows):
        pairs = []
        for s in range(plan.span):
            columns = slice(s * PAIR, (s + 1) * PAIR)
            both = dot(terms[:, columns], rows[:, columns], outer)
            pairs.append(jnp.where(first, both[:TILE], both[TILE:]))
        return jnp.concatenate(pairs, axis=1)

    def spans(p):
        offset = p * lanes
        start = plan.chunk_starts[g] * PAIR + offset
        if not isinstance(p, int):
            offset, start = pl.multiple_of(offset, lanes), pl.multiple_of(start, PAIR)
        here = pl.ds(pl.multiple_of(me * plan.cols + start, PAIR), lanes)
        there = pl.ds(piece_start(plan, me, start), lanes)
        span = pl.ds(offset, lanes)
        cut = pl.ds(start, lanes)
        return here, there, cut, span, cut if last else span

    def prepare(p, b):
        here, there, _, span, _ = spans(p)
        for a, scratch in enumerate((k_s, v_s)):
            for i in range(per):
                rows = pl.ds(i * TILE, TILE)
                scratch[b, i] = own[1 + a][rows, here]
                for r in range(1, members):
                    scratch[b, r * per + i] = key_value[(r - 1) * 2 + a][rows, there]
            for far in range(2):
                for i in range(remote):
                    scratch[b, tiles + far * remote + i] = borders[far][a, i, :, span]
        dk_s[b] = jnp.zeros(dk_s.shape[1:], dk_s.dtype)
        dv_s[b] = jnp.zeros(dv_s.shape[1:], dv_s.dtype)

    def first_products(p, b, t):
        here, _, cut, _, _ = spans(p)

        def load(a):
            rows = pl.ds(t % per * TILE, TILE)
            if t < per:
                return own[a][rows, here]
            return query_grad[(t // per - 1) * 2 + a // 3][rows, cut]

        at = [slots[t, j] for j in range(width)]
        queries = apart(load(0) * jnp.bfloat16(scale))
        grads = apart(load(3))
        keys = jnp.concatenate([k_s[b, s] for s in at], axis=0)
        values = jnp.concatenate([v_s[b, s] for s in at], axis=0)
        return at, queries, grads, keys, values, dot(keys, queries, inner), dot(values, grads, inner)

    def softmax(t, scores, grad_probs):
        masked = jnp.concatenate(
            [jnp.where(j < live[t], scores[j * TILE : (j + 1) * TILE], NEG) for j in range(width)], axis=0
        )
        terms = jnp.exp(masked - jnp.max(masked, axis=0, keepdims=True))
        probs = terms * (1.0 / jnp.sum(terms, axis=0, keepdims=True))
        delta = jnp.sum(probs * grad_probs, axis=0, keepdims=True)
        return probs.astype(jnp.bfloat16), (probs * (grad_probs - delta)).astype(jnp.bfloat16)

    def second_products(p, b, t, at, queries, grads, keys, values, probs_low, grad_low):
        result = spans(p)[-1]
        rows = pl.ds(t % per * TILE, TILE)
        out = outs[t // per]
        out[0, rows, result] = together(probs_low, values).astype(jnp.bfloat16)
        out[1, rows, result] = (together(grad_low, keys) * scale).astype(jnp.bfloat16)
        key_part = dot(grad_low, queries, natural)
        value_part = dot(probs_low, grads, natural)
        for j, s in enumerate(at):
            dk_s[b, s] += key_part[j * TILE : (j + 1) * TILE]
            dv_s[b, s] += value_part[j * TILE : (j + 1) * TILE]

    def finish(p, b):
        _, _, _, span, result = spans(p)
        for a, scratch in enumerate((dk_s, dv_s)):
            for t in range(tiles):
                rows = pl.ds(t % per * TILE, TILE)
                outs[t // per][2 + a, rows, result] = scratch[b, t].astype(jnp.bfloat16)
            for far in range(2):
                for i in range(remote):
                    parts[far][a, i, :, span] = scratch[b, tiles + far * remote + i].astype(jnp.bfloat16)

    def some_blocks(places):
        steps = [(p, b, t) for b, p in enumerate(places) for t in range(tiles)]
        products, weights = {}, {}
        for n in range(len(steps) + 2):
            if n < len(steps):
                p, b, t = steps[n]
                if t == 0:
                    prepare(p, b)
                products[n] = first_products(p, b, t)
            if 0 <= n - 1 < len(steps):
                weights[n - 1] = softmax(steps[n - 1][2], *products[n - 1][5:])
            if 0 <= n - 2:
                p, b, t = steps[n - 2]
                second_products(p, b, t, *products.pop(n - 2)[:5], *weights.pop(n - 2))
                if t == tiles - 1:
                    finish(p, b)

    if plan.unrolled == plan.blocks[g]:
        some_blocks(range(plan.blocks[g]))
    else:
        lax.fori_loop(0, plan.blocks[g], lambda p, carry: (some_blocks([p]), carry)[1], 0)


def write_out(scratch, outs, sem, fill):
    copies = []
    for a in range(2):
        for i in range(outs[a].shape[0] // TILE):
            rows = pl.ds(i * TILE, TILE)
            fill(a, i, rows)
            slot = len(copies)
            copies.append(pltpu.make_async_copy(scratch.at[a, rows, :], outs[a].at[rows, :], sem.at[slot]))
            copies[-1].start()
    for copy in copies:
        copy.wait()


def join_kernel(plan, *refs):
    members, outs, scratch, sem = plan.members, refs[-4:-2], refs[-2], refs[-1]
    _, me = position(plan)

    def fill(a, i, rows):
        for r in range(members):
            start = pl.multiple_of((me + r) % members * plan.cols, PAIR)
            scratch[a, rows, pl.ds(start, plan.cols)] = refs[r][a, rows, :]

    write_out(scratch, outs, sem, fill)


def add_kernel(plan, lists_ref, counts_ref, *refs):
    members, outs, scratch, sem = plan.members, refs[-4:-2], refs[-2], refs[-1]
    pieces, borders = refs[:members], refs[members:-4]
    frame, me = position(plan)
    partners = [partner(frame, far) for far in range(2)]
    picks = [listed(plan, lists_ref, counts_ref, other, frame) for other in partners]

    def fill(a, i, rows):
        hits = []
        for far in range(2):
            exists = (partners[far] >= 0) & (partners[far] < plan.frames)
            for j, pick in enumerate(picks[far]):
                hits.append((far, j, exists & (pick == me * plan.device_tiles + i)))
        for r in range(members):
            start = pl.multiple_of((me + r) % members * plan.cols, PAIR)
            scratch[a, rows, pl.ds(start, plan.cols)] = pieces[r][2 + a, rows, :]

        @pl.when(functools.reduce(lambda x, y: x | y, [hit for _, _, hit in hits]))
        def _():
            for g, count in enumerate(plan.chunk_pairs):
                for r in range(members):
                    columns = pl.ds(plan.chunk_starts[g] * PAIR, count * PAIR)
                    start = (me + r) % members * plan.cols + plan.chunk_starts[g] * PAIR
                    total = pieces[r][2 + a, rows, columns].astype(jnp.float32)
                    for far, j, hit in hits:
                        border = borders[(g * members + r) * 2 + far]
                        total += jnp.where(hit, border[a, j].astype(jnp.float32), 0.0)
                    span = pl.ds(pl.multiple_of(start, PAIR), count * PAIR)
                    scratch[a, rows, span] = total.astype(jnp.bfloat16)

    write_out(scratch, outs, sem, fill)


def per_device(queries, key_vectors, value_vectors, grad_out, key_tiles, tile_counts):
    rows, width = queries.shape
    plan = Plan(rows, width, key_tiles.shape[1])
    members, remote, chunks = plan.members, plan.remote, len(plan.chunk_pairs)
    axes = ("ulysses", "tm")
    lists = key_tiles.T
    low = jnp.bfloat16
    scalars = pl.BlockSpec(memory_space=pltpu.SMEM)
    whole = pl.BlockSpec(memory_space=pltpu.VMEM)
    anywhere = pl.BlockSpec(memory_space=pl.ANY)
    shape = jax.ShapeDtypeStruct
    params = pltpu.CompilerParams(vmem_limit_bytes=VMEM_LIMIT)

    def cost(moved, flops=0, terms=0):
        return pl.CostEstimate(flops=flops, bytes_accessed=moved, transcendentals=terms)

    def exchange(name, whole_rows, after, *sources):
        if plan.whole_pieces and whole_rows:
            return [lax.ppermute(x, axes, plan.member_perm(1)) for x in sources]
        places = (members - 1) * len(sources) * (rows // BLOCK)
        direct = not plan.whole_pieces
        after = [] if direct else after
        kernel = functools.partial(split_kernel, plan) if direct else functools.partial(slice_kernel, plan, len(after))
        sends = pl.pallas_call(
            kernel,
            out_shape=[shape((rows, plan.cols), low)] * (members - 1) * len(sources),
            in_specs=[anywhere] * len(after) + [anywhere if direct else whole] * len(sources),
            out_specs=[whole] * (members - 1) * len(sources),
            scratch_shapes=[pltpu.SemaphoreType.DMA((places,))] if direct else [],
            compiler_params=params,
            cost_estimate=cost(4 * len(sources) * rows * width),
            name=name,
        )(*after, *[pltpu.with_memory_space_constraint(x, pltpu.HBM) if direct else x for x in sources])
        each = len(sources)
        return [lax.ppermute(x, axes, plan.member_perm(1 + n // each)) for n, x in enumerate(sends)]

    key_value = exchange("split_kv", True, [], key_vectors, value_vectors)

    def hold_kernel(after, *refs):
        refs = refs[after:]
        for source, out in zip(refs[: len(refs) // 2], refs[len(refs) // 2 :], strict=True):
            out[...] = source[...]

    def hold(name, after, *sources):
        return pl.pallas_call(
            functools.partial(hold_kernel, len(after)),
            out_shape=[shape(x.shape, low) for x in sources],
            in_specs=[anywhere] * len(after) + [whole] * len(sources),
            out_specs=[whole] * len(sources),
            compiler_params=params,
            cost_estimate=cost(4 * sum(x.size for x in sources)),
            name=name,
        )(*after, *sources)

    arrived = []
    for g, count in enumerate(plan.chunk_pairs):
        picked = pl.pallas_call(
            functools.partial(pick_kernel, plan, g),
            out_shape=[shape((2, remote, TILE, count * PAIR), low)] * 2,
            in_specs=[scalars] * 2 + [whole] * (2 * members),
            out_specs=[whole] * 2,
            compiler_params=params,
            cost_estimate=cost(16 * remote * TILE * count * PAIR),
            name=f"pick_{g}",
        )(lists, tile_counts, key_vectors, value_vectors, *key_value)
        near, far = picked
        if g > 0:
            [near] = hold(f"hold_near_{g}", [arrived[-1][0]], near)
        arrived.append([lax.ppermute(x, axes, plan.frame_perm(i)) for i, x in enumerate((near, far))])
    query_grad = exchange("split_qg", False, [], queries, grad_out)

    def home(sent, r):
        return lax.ppermute(sent, axes, plan.member_perm(members - r))

    earlier, border_terms, nears, fars = [], [], [], []
    for g, count in enumerate(plan.chunk_pairs):
        cols = count * PAIR
        wide = plan.cols if g == chunks - 1 else cols
        scores = plan.frame_tiles * plan.list_width * TILE * 2 * TILE * count
        outs = pl.pallas_call(
            functools.partial(attend_kernel, plan, g),
            out_shape=[shape((4, rows, wide), low)] * members + [shape((2, remote, TILE, cols), low)] * 2,
            in_specs=[scalars] * 2 + [whole] * (4 + 4 * (members - 1) + 2 + len(earlier)),
            out_specs=[whole] * (members + 2),
            scratch_shapes=[
                pltpu.VMEM((plan.unrolled, plan.ext_tiles, TILE, plan.lanes), low),
                pltpu.VMEM((plan.unrolled, plan.ext_tiles, TILE, plan.lanes), low),
                pltpu.VMEM((plan.unrolled, plan.ext_tiles, TILE, plan.lanes), jnp.float32),
                pltpu.VMEM((plan.unrolled, plan.ext_tiles, TILE, plan.lanes), jnp.float32),
                pltpu.SMEM((plan.frame_tiles, plan.list_width), jnp.int32),
            ],
            compiler_params=params,
            cost_estimate=cost(16 * members * rows * cols, 12 * scores * PAIR, scores),
            name=f"attend_{g}",
        )(
            lists, tile_counts, queries, key_vectors, value_vectors, grad_out,
            *key_value, *query_grad, *arrived[g], *earlier,
        )
        parts = list(outs[members:])
        earlier += outs[:members]
        if g > 0:
            held = hold(f"hold_far_{g}", [nears[-1], fars[-1]], parts[1], *earlier[1 - members :])
            parts[1], earlier[1 - members :] = held[0], held[1:]
        nears.append(lax.ppermute(parts[0], axes, plan.frame_perm(0)))
        fars.append(lax.ppermute(parts[1], axes, plan.frame_perm(1)))
    for near, far in zip(nears, fars, strict=True):
        border_terms += [near, far]
        for r in range(1, members):
            border_terms += [home(near, r), home(far, r)]
    pieces = [earlier[-members], *[home(earlier[r - members], r) for r in range(1, members)]]

    attended, grad_queries = pl.pallas_call(
        functools.partial(join_kernel, plan),
        out_shape=[shape((rows, width), low)] * 2,
        in_specs=[whole] * members,
        out_specs=[pl.BlockSpec(memory_space=pltpu.HBM)] * 2,
        scratch_shapes=[pltpu.VMEM((2, rows, width), low), pltpu.SemaphoreType.DMA((2 * plan.device_tiles,))],
        compiler_params=params,
        cost_estimate=cost(8 * rows * width),
        name="join",
    )(*pieces)
    grad_keys, grad_values = pl.pallas_call(
        functools.partial(add_kernel, plan),
        out_shape=[shape((rows, width), low)] * 2,
        in_specs=[scalars] * 2 + [whole] * (members + len(border_terms)),
        out_specs=[pl.BlockSpec(memory_space=pltpu.HBM)] * 2,
        scratch_shapes=[pltpu.VMEM((2, rows, width), low), pltpu.SemaphoreType.DMA((2 * plan.device_tiles,))],
        compiler_params=params,
        cost_estimate=cost(10 * rows * width),
        name="add",
    )(lists, tile_counts, *pieces, *border_terms)
    return attended, grad_queries, grad_keys, grad_values


def solution(mesh):
    tokens = P(("clips", "tm", "ulysses"), None)
    return jax.shard_map(
        per_device,
        mesh=mesh,
        in_specs=(tokens, tokens, tokens, tokens, P("clips", None), P("clips")),
        out_specs=(tokens, tokens, tokens, tokens),
        check_vma=False,
    )
```

profile of v0, /device:TPU:21, one launch (start us, length us, event | category | flops | bytes accessed | tf_op | source)
XLA Modules:
  0.0 51.4 jit_solution(2758373607050471242)
XLA Ops:
  0.6 0.0 copy-start
  0.6 0.0 copy-start.1
  0.7 0.7 %collective-permute-start = (bf16[128,3072]{1,0:T(8,128)(2,1)}, bf16[128,3072]{1,0:T(8,128)(2,1)S(1)}, u32[]{:S(2)}, u32[]{:S(2)}) collective-permute-start(bf16[128,3072]{1,0:T(8,128)(2,1)} %refs_1_.9), channel_id=1, source_target_pairs={{0,4},{4,0},{8,12},{12,8},{1,5},{5,1},{9,13},{13,9},{2,6},{6,2},{1... | collective-permute-start | bytes 2359304 | tf_op jit(solution)/shard_map/ppermute | solution.py:396
  1.4 0.1 collective-permute-start.1
  1.5 1.1 %copy-done.2 = bf16[128,3072]{1,0:T(8,128)(2,1)S(1)} copy-done((bf16[128,3072]{1,0:T(8,128)(2,1)S(1)}, bf16[128,3072]{1,0:T(8,128)(2,1)}, u32[]{:S(2)}) %copy-start.2) | copy-done | bytes 786456
  2.6 1.1 %copy-done.4 = bf16[128,3072]{1,0:T(8,128)(2,1)S(1)} copy-done((bf16[128,3072]{1,0:T(8,128)(2,1)S(1)}, bf16[128,3072]{1,0:T(8,128)(2,1)}, u32[]{:S(2)}) %copy-start.4) | copy-done | bytes 786456
  3.7 0.1 split_qg.1
  3.8 0.5 collective-permute-start.2
  4.3 0.1 collective-permute-start.3
  4.4 0.0 collective-permute-done.refs_2_.refs_4_
  4.4 0.3 collective-permute-done.1.refs_3_.refs_5_
  4.6 0.0 copy-done.6
  4.7 0.7 %pick_0.1 = (bf16[2,1,64,768]{3,2,1,0:T(8,128)(2,1)S(1)}, bf16[2,1,64,768]{3,2,1,0:T(8,128)(2,1)S(1)}) custom-call(s32[3,32]{1,0:T(4,128)S(1)} %bitcast.1, s32[32]{0:T(128)S(1)} %copy-done.6, bf16[128,3072]{1,0:T(8,128)(2,1)S(1)} %copy-done, bf16[128,3072]{1,0:T(8,128)(2,1)S(1)} %copy-done.1, bf16[128,3072]{1,0:T(8,128)(2,1)S(1)} %collective-permute-done.refs_2_.refs_4_, ...), custom_call_target="tpu_custom_call" | custom-call | bytes 786432 | tf_op jit(solution)/shard_map/pick_0/pallas_call | solution.py:434
  5.4 0.3 collective-permute-start.4
  5.7 4.3 %collective-permute-start.7 = (bf16[2,1,64,768]{3,2,1,0:T(8,128)(2,1)S(1)}, bf16[2,1,64,768]{3,2,1,0:T(8,128)(2,1)S(1)}, u32[]{:S(2)}, u32[]{:S(2)}) collective-permute-start(bf16[2,1,64,768]{3,2,1,0:T(8,128)(2,1)S(1)} %get-tuple-element.29), channel_id=1, source_target_pairs={{8,1},{12,5},{1,8},{5,12},{9,2},{13,6},{2,9},{6,13},{10,3},{14,7},... | collective-permute-start | bytes 589832 | tf_op jit(solution)/shard_map/ppermute | solution.py:446
  10.0 0.7 %pick_1.1 = (bf16[2,1,64,768]{3,2,1,0:T(8,128)(2,1)S(1)}, bf16[2,1,64,768]{3,2,1,0:T(8,128)(2,1)S(1)}) custom-call(s32[3,32]{1,0:T(4,128)S(1)} %bitcast.2, s32[32]{0:T(128)S(1)} %copy-done.6, bf16[128,3072]{1,0:T(8,128)(2,1)S(1)} %copy-done, bf16[128,3072]{1,0:T(8,128)(2,1)S(1)} %copy-done.1, bf16[128,3072]{1,0:T(8,128)(2,1)S(1)} %collective-permute-done.refs_2_.refs_4_, ...), custom_call_target="tpu_custom_call" | custom-call | bytes 786432 | tf_op jit(solution)/shard_map/pick_1/pallas_call | solution.py:434
  10.8 2.0 %collective-permute-start.6 = (bf16[2,1,64,768]{3,2,1,0:T(8,128)(2,1)S(1)}, bf16[2,1,64,768]{3,2,1,0:T(8,128)(2,1)S(1)}, u32[]{:S(2)}, u32[]{:S(2)}) collective-permute-start(bf16[2,1,64,768]{3,2,1,0:T(8,128)(2,1)S(1)} %get-tuple-element.28), channel_id=1, source_target_pairs={{8,1},{12,5},{1,8},{5,12},{9,2},{13,6},{2,9},{6,13},{10,3},{14,7},... | collective-permute-start | bytes 589832 | tf_op jit(solution)/shard_map/ppermute | solution.py:446
  12.8 3.0 %collective-permute-done.4.refs_0_.refs_8_ = bf16[2,1,64,768]{3,2,1,0:T(8,128)(2,1)S(1)} collective-permute-done((bf16[2,1,64,768]{3,2,1,0:T(8,128)(2,1)S(1)}, bf16[2,1,64,768]{3,2,1,0:T(8,128)(2,1)S(1)}, u32[]{:S(2)}, u32[]{:S(2)}) %collective-permute-start.4) | collective-permute-done | bytes 196640 | tf_op jit(solution)/shard_map/ppermute | solution.py:446
  15.8 0.1 collective-permute-start.5
  15.9 0.0 collective-permute-done.2.refs_6_
  15.9 0.0 collective-permute-done.3.refs_7_
  15.9 0.0 collective-permute-done.7.refs_9_
  15.9 0.0 copy-done.3
  15.9 4.1 %attend_0.1 = (bf16[4,128,768]{2,1,0:T(8,128)(2,1)S(1)}, bf16[4,128,768]{2,1,0:T(8,128)(2,1)S(1)}, bf16[2,1,64,768]{3,2,1,0:T(8,128)(2,1)S(1)}, bf16[2,1,64,768]{3,2,1,0:T(8,128)(2,1)S(1)}) custom-call(s32[3,32]{1,0:T(4,128)S(1)} %bitcast.3, s32[32]{0:T(128)S(1)} %copy-done.6, bf16[128,3072]{1,0:T(8,128)(2,1)S(1)} %copy-done.3, ...), custom_call_target="tpu_custom_call" | custom-call | flops 905969664 | bytes 3145728 | tf_op jit(solution)/shard_map/attend_0/pallas_call | solution.py:457
  20.0 1.5 %collective-permute-start.8 = (bf16[2,1,64,768]{3,2,1,0:T(8,128)(2,1)S(1)}, bf16[2,1,64,768]{3,2,1,0:T(8,128)(2,1)S(1)}, u32[]{:S(2)}, u32[]{:S(2)}) collective-permute-start(bf16[2,1,64,768]{3,2,1,0:T(8,128)(2,1)S(1)} %get-tuple-element.33), channel_id=1, source_target_pairs={{0,8},{4,12},{8,0},{12,4},{1,9},{5,13},{9,1},{13,5},{2,10},{6,14},... | collective-permute-start | bytes 589832 | tf_op jit(solution)/shard_map/ppermute | solution.py:481
  21.5 1.9 %collective-permute-start.9 = (bf16[2,1,64,768]{3,2,1,0:T(8,128)(2,1)S(1)}, bf16[2,1,64,768]{3,2,1,0:T(8,128)(2,1)S(1)}, u32[]{:S(2)}, u32[]{:S(2)}) collective-permute-start(bf16[2,1,64,768]{3,2,1,0:T(8,128)(2,1)S(1)} %get-tuple-element.34), channel_id=1, source_target_pairs={{8,1},{12,5},{1,8},{5,12},{9,2},{13,6},{2,9},{6,13},{10,3},{14,7},... | collective-permute-start | bytes 589832 | tf_op jit(solution)/shard_map/ppermute | solution.py:482
  23.4 0.0 collective-permute-done.6.refs_9_
  23.4 0.0 collective-permute-done.5.refs_8_
  23.4 4.1 %attend_1.1 = (bf16[4,128,1536]{2,1,0:T(8,128)(2,1)S(1)}, bf16[4,128,1536]{2,1,0:T(8,128)(2,1)S(1)}, bf16[2,1,64,768]{3,2,1,0:T(8,128)(2,1)S(1)}, bf16[2,1,64,768]{3,2,1,0:T(8,128)(2,1)S(1)}) custom-call(s32[3,32]{1,0:T(4,128)S(1)} %bitcast.4, s32[32]{0:T(128)S(1)} %copy-done.6, bf16[128,3072]{1,0:T(8,128)(2,1)S(1)} %copy-done.3, ...), custom_call_target="tpu_custom_call" | custom-call | flops 905969664 | bytes 3145728 | tf_op jit(solution)/shard_map/attend_1/pallas_call | solution.py:457
  27.6 0.6 %collective-permute-done.8.refs_0_.refs_2_ = bf16[2,1,64,768]{3,2,1,0:T(8,128)(2,1)S(1)} collective-permute-done((bf16[2,1,64,768]{3,2,1,0:T(8,128)(2,1)S(1)}, bf16[2,1,64,768]{3,2,1,0:T(8,128)(2,1)S(1)}, u32[]{:S(2)}, u32[]{:S(2)}) %collective-permute-start.8) | collective-permute-done | bytes 196640 | tf_op jit(solution)/shard_map/ppermute | solution.py:481
  28.1 0.8 %collective-permute-done.9.refs_1_.refs_3_ = bf16[2,1,64,768]{3,2,1,0:T(8,128)(2,1)S(1)} collective-permute-done((bf16[2,1,64,768]{3,2,1,0:T(8,128)(2,1)S(1)}, bf16[2,1,64,768]{3,2,1,0:T(8,128)(2,1)S(1)}, u32[]{:S(2)}, u32[]{:S(2)}) %collective-permute-start.9) | collective-permute-done | bytes 196640 | tf_op jit(solution)/shard_map/ppermute | solution.py:482
  28.9 0.1 hold_far_1.1
  29.0 7.3 %collective-permute-start.10 = (bf16[4,128,1536]{2,1,0:T(8,128)(2,1)S(1)}, bf16[4,128,1536]{2,1,0:T(8,128)(2,1)S(1)}, u32[]{:S(2)}, u32[]{:S(2)}) collective-permute-start(bf16[4,128,1536]{2,1,0:T(8,128)(2,1)S(1)} %get-tuple-element.37), channel_id=1, source_target_pairs={{0,4},{4,0},{8,12},{12,8},{1,5},{5,1},{9,13},{13,9},{2,6},{6,2},{1... | collective-permute-start | bytes 4718600 | tf_op jit(solution)/shard_map/ppermute | solution.py:450
  36.3 0.0 collective-permute-start.13
  36.3 2.2 %collective-permute-start.14 = (bf16[2,1,64,768]{3,2,1,0:T(8,128)(2,1)S(1)}, bf16[2,1,64,768]{3,2,1,0:T(8,128)(2,1)S(1)}, u32[]{:S(2)}, u32[]{:S(2)}) collective-permute-start(bf16[2,1,64,768]{3,2,1,0:T(8,128)(2,1)S(1)} %get-tuple-element.41), channel_id=1, source_target_pairs={{8,1},{12,5},{1,8},{5,12},{9,2},{13,6},{2,9},{6,13},{10,3},{14,7},... | collective-permute-start | bytes 589832 | tf_op jit(solution)/shard_map/ppermute | solution.py:482
  38.5 0.4 collective-permute-start.11
  39.0 0.1 collective-permute-start.12
  39.1 7.9 %collective-permute-done.13.refs_6_ = bf16[2,1,64,768]{3,2,1,0:T(8,128)(2,1)S(1)} collective-permute-done((bf16[2,1,64,768]{3,2,1,0:T(8,128)(2,1)S(1)}, bf16[2,1,64,768]{3,2,1,0:T(8,128)(2,1)S(1)}, u32[]{:S(2)}, u32[]{:S(2)}) %collective-permute-start.13) | collective-permute-done | bytes 196640 | tf_op jit(solution)/shard_map/ppermute | solution.py:481
  47.0 0.8 %collective-permute-start.15 = (bf16[2,1,64,768]{3,2,1,0:T(8,128)(2,1)S(1)}, bf16[2,1,64,768]{3,2,1,0:T(8,128)(2,1)S(1)}, u32[]{:S(2)}, u32[]{:S(2)}) collective-permute-start(bf16[2,1,64,768]{3,2,1,0:T(8,128)(2,1)S(1)} %collective-permute-done.13.refs_6_), channel_id=1, source_target_pairs={{0,4},{4,0},{8,12},{12,8},{1,5},{5,1},{9,13},{13,9},{2,6},{6,2},{1... | collective-permute-start | bytes 589832 | tf_op jit(solution)/shard_map/ppermute | solution.py:450
  47.9 0.0 collective-permute-done.14.refs_7_
  47.9 0.0 collective-permute-start.16
  47.9 0.0 collective-permute-done.10.refs_1_
  47.9 1.2 %join.1 = (bf16[128,3072]{1,0:T(8,128)(2,1)}, bf16[128,3072]{1,0:T(8,128)(2,1)}) custom-call(bf16[4,128,1536]{2,1,0:T(8,128)(2,1)S(1)} %get-tuple-element.32.refs_0_, bf16[4,128,1536]{2,1,0:T(8,128)(2,1)S(1)} %collective-permute-done.10.refs_1_), custom_call_target="tpu_custom_call" | custom-call | bytes 3145728 | tf_op jit(solution)/shard_map/join/pallas_call | solution.py:489
  49.1 0.0 collective-permute-done.11.refs_4_
  49.1 0.0 collective-permute-done.12.refs_5_
  49.1 0.0 collective-permute-done.15.refs_8_
  49.1 0.2 collective-permute-done.16.refs_9_
  49.3 2.1 %add.1 = (bf16[128,3072]{1,0:T(8,128)(2,1)}, bf16[128,3072]{1,0:T(8,128)(2,1)}) custom-call(s32[3,32]{1,0:T(4,128)S(1)} %bitcast.5, s32[32]{0:T(128)S(1)} %copy-done.6, bf16[4,128,1536]{2,1,0:T(8,128)(2,1)S(1)} %get-tuple-element.32.refs_0_, bf16[4,128,1536]{2,1,0:T(8,128)(2,1)S(1)} %collective-permute-done.10.refs_1_, ...), custom_call_target="tpu_custom_call" | custom-call | bytes 3932160 | tf_op jit(solution)/shard_map/add/pallas_call | solution.py:499
  (9 shorter events, 0.0 us)
Async XLA Ops:
  0.6 4.0 %copy-start = (bf16[128,3072]{1,0:T(8,128)(2,1)S(1)}, bf16[128,3072]{1,0:T(8,128)(2,1)}, u32[]{:S(2)}) copy-start(bf16[128,3072]{1,0:T(8,128)(2,1)} %refs_1_.9) | copy-start | bytes 2359300
  0.6 4.0 %copy-start.1 = (bf16[128,3072]{1,0:T(8,128)(2,1)S(1)}, bf16[128,3072]{1,0:T(8,128)(2,1)}, u32[]{:S(2)}) copy-start(bf16[128,3072]{1,0:T(8,128)(2,1)} %refs_2_.3) | copy-start | bytes 2359300
  0.7 3.7 %collective-permute-start = (bf16[128,3072]{1,0:T(8,128)(2,1)}, bf16[128,3072]{1,0:T(8,128)(2,1)S(1)}, u32[]{:S(2)}, u32[]{:S(2)}) collective-permute-start(bf16[128,3072]{1,0:T(8,128)(2,1)} %refs_1_.9), channel_id=1, source_target_pairs={{0,4},{4,0},{8,12},{12,8},{1,5},{5,1},{9,13},{13,9},{2,6},{6,2},{1... | collective-permute-start | bytes 2359304 | tf_op jit(solution)/shard_map/ppermute | solution.py:396
  1.4 3.2 %collective-permute-start.1 = (bf16[128,3072]{1,0:T(8,128)(2,1)}, bf16[128,3072]{1,0:T(8,128)(2,1)S(1)}, u32[]{:S(2)}, u32[]{:S(2)}) collective-permute-start(bf16[128,3072]{1,0:T(8,128)(2,1)} %refs_2_.3), channel_id=1, source_target_pairs={{0,4},{4,0},{8,12},{12,8},{1,5},{5,1},{9,13},{13,9},{2,6},{6,2},{1... | collective-permute-start | bytes 2359304 | tf_op jit(solution)/shard_map/ppermute | solution.py:396
  1.5 1.1 %copy-start.2 = (bf16[128,3072]{1,0:T(8,128)(2,1)S(1)}, bf16[128,3072]{1,0:T(8,128)(2,1)}, u32[]{:S(2)}) copy-start(bf16[128,3072]{1,0:T(8,128)(2,1)} %refs_0_.9) | copy-start | bytes 2359300
  2.6 1.1 %copy-start.4 = (bf16[128,3072]{1,0:T(8,128)(2,1)S(1)}, bf16[128,3072]{1,0:T(8,128)(2,1)}, u32[]{:S(2)}) copy-start(bf16[128,3072]{1,0:T(8,128)(2,1)} %refs_3_.3) | copy-start | bytes 2359300
  3.7 0.9 %copy-start.5 = (s32[32,3]{0,1:T(4,128)S(1)}, s32[32,3]{0,1:T(4,128)}, u32[]{:S(2)}) copy-start(s32[32,3]{0,1:T(4,128)} %param.10) | copy-start | bytes 1156
  3.7 0.9 %copy-start.6 = (s32[32]{0:T(128)S(1)}, s32[32]{0:T(128)}, u32[]{:S(2)}) copy-start(s32[32]{0:T(128)} %counts_ref.9) | copy-start | bytes 388
  3.8 12.1 %collective-permute-start.2 = (bf16[128,1536]{1,0:T(8,128)(2,1)S(1)}, bf16[128,1536]{1,0:T(8,128)(2,1)S(1)}, u32[]{:S(2)}, u32[]{:S(2)}) collective-permute-start(bf16[128,1536]{1,0:T(8,128)(2,1)S(1)} %get-tuple-element.24), channel_id=1, source_target_pairs={{0,4},{4,0},{8,12},{12,8},{1,5},{5,1},{9,13},{13,9},{2,6},{6,2},{1... | collective-permute-start | bytes 1179656 | tf_op jit(solution)/shard_map/ppermute | solution.py:412
  4.3 11.6 %collective-permute-start.3 = (bf16[128,1536]{1,0:T(8,128)(2,1)S(1)}, bf16[128,1536]{1,0:T(8,128)(2,1)S(1)}, u32[]{:S(2)}, u32[]{:S(2)}) collective-permute-start(bf16[128,1536]{1,0:T(8,128)(2,1)S(1)} %get-tuple-element.25), channel_id=1, source_target_pairs={{0,4},{4,0},{8,12},{12,8},{1,5},{5,1},{9,13},{13,9},{2,6},{6,2},{1... | collective-permute-start | bytes 1179656 | tf_op jit(solution)/shard_map/ppermute | solution.py:412
  5.4 10.4 %collective-permute-start.4 = (bf16[2,1,64,768]{3,2,1,0:T(8,128)(2,1)S(1)}, bf16[2,1,64,768]{3,2,1,0:T(8,128)(2,1)S(1)}, u32[]{:S(2)}, u32[]{:S(2)}) collective-permute-start(bf16[2,1,64,768]{3,2,1,0:T(8,128)(2,1)S(1)} %get-tuple-element.26), channel_id=1, source_target_pairs={{0,8},{4,12},{8,0},{12,4},{1,9},{5,13},{9,1},{13,5},{2,10},{6,14},... | collective-permute-start | bytes 589832 | tf_op jit(solution)/shard_map/ppermute | solution.py:446
  5.7 10.2 %copy-start.3 = (bf16[128,3072]{1,0:T(8,128)(2,1)S(1)}, bf16[128,3072]{1,0:T(8,128)(2,1)}, u32[]{:S(2)}) copy-start(bf16[128,3072]{1,0:T(8,128)(2,1)} %refs_0_.9) | copy-start | bytes 2359300
  5.7 10.2 %collective-permute-start.7 = (bf16[2,1,64,768]{3,2,1,0:T(8,128)(2,1)S(1)}, bf16[2,1,64,768]{3,2,1,0:T(8,128)(2,1)S(1)}, u32[]{:S(2)}, u32[]{:S(2)}) collective-permute-start(bf16[2,1,64,768]{3,2,1,0:T(8,128)(2,1)S(1)} %get-tuple-element.29), channel_id=1, source_target_pairs={{8,1},{12,5},{1,8},{5,12},{9,2},{13,6},{2,9},{6,13},{10,3},{14,7},... | collective-permute-start | bytes 589832 | tf_op jit(solution)/shard_map/ppermute | solution.py:446
  10.8 12.7 %collective-permute-start.6 = (bf16[2,1,64,768]{3,2,1,0:T(8,128)(2,1)S(1)}, bf16[2,1,64,768]{3,2,1,0:T(8,128)(2,1)S(1)}, u32[]{:S(2)}, u32[]{:S(2)}) collective-permute-start(bf16[2,1,64,768]{3,2,1,0:T(8,128)(2,1)S(1)} %get-tuple-element.28), channel_id=1, source_target_pairs={{8,1},{12,5},{1,8},{5,12},{9,2},{13,6},{2,9},{6,13},{10,3},{14,7},... | collective-permute-start | bytes 589832 | tf_op jit(solution)/shard_map/ppermute | solution.py:446
  15.8 7.6 %collective-permute-start.5 = (bf16[2,1,64,768]{3,2,1,0:T(8,128)(2,1)S(1)}, bf16[2,1,64,768]{3,2,1,0:T(8,128)(2,1)S(1)}, u32[]{:S(2)}, u32[]{:S(2)}) collective-permute-start(bf16[2,1,64,768]{3,2,1,0:T(8,128)(2,1)S(1)} %hold_near_1.1), channel_id=1, source_target_pairs={{0,8},{4,12},{8,0},{12,4},{1,9},{5,13},{9,1},{13,5},{2,10},{6,14},... | collective-permute-start | bytes 589832 | tf_op jit(solution)/shard_map/ppermute | solution.py:446
  20.0 8.1 %collective-permute-start.8 = (bf16[2,1,64,768]{3,2,1,0:T(8,128)(2,1)S(1)}, bf16[2,1,64,768]{3,2,1,0:T(8,128)(2,1)S(1)}, u32[]{:S(2)}, u32[]{:S(2)}) collective-permute-start(bf16[2,1,64,768]{3,2,1,0:T(8,128)(2,1)S(1)} %get-tuple-element.33), channel_id=1, source_target_pairs={{0,8},{4,12},{8,0},{12,4},{1,9},{5,13},{9,1},{13,5},{2,10},{6,14},... | collective-permute-start | bytes 589832 | tf_op jit(solution)/shard_map/ppermute | solution.py:481
  21.5 7.4 %collective-permute-start.9 = (bf16[2,1,64,768]{3,2,1,0:T(8,128)(2,1)S(1)}, bf16[2,1,64,768]{3,2,1,0:T(8,128)(2,1)S(1)}, u32[]{:S(2)}, u32[]{:S(2)}) collective-permute-start(bf16[2,1,64,768]{3,2,1,0:T(8,128)(2,1)S(1)} %get-tuple-element.34), channel_id=1, source_target_pairs={{8,1},{12,5},{1,8},{5,12},{9,2},{13,6},{2,9},{6,13},{10,3},{14,7},... | collective-permute-start | bytes 589832 | tf_op jit(solution)/shard_map/ppermute | solution.py:482
  29.0 18.8 %collective-permute-start.10 = (bf16[4,128,1536]{2,1,0:T(8,128)(2,1)S(1)}, bf16[4,128,1536]{2,1,0:T(8,128)(2,1)S(1)}, u32[]{:S(2)}, u32[]{:S(2)}) collective-permute-start(bf16[4,128,1536]{2,1,0:T(8,128)(2,1)S(1)} %get-tuple-element.37), channel_id=1, source_target_pairs={{0,4},{4,0},{8,12},{12,8},{1,5},{5,1},{9,13},{13,9},{2,6},{6,2},{1... | collective-permute-start | bytes 4718600 | tf_op jit(solution)/shard_map/ppermute | solution.py:450
  36.3 10.7 %collective-permute-start.13 = (bf16[2,1,64,768]{3,2,1,0:T(8,128)(2,1)S(1)}, bf16[2,1,64,768]{3,2,1,0:T(8,128)(2,1)S(1)}, u32[]{:S(2)}, u32[]{:S(2)}) collective-permute-start(bf16[2,1,64,768]{3,2,1,0:T(8,128)(2,1)S(1)} %get-tuple-element.40), channel_id=1, source_target_pairs={{0,8},{4,12},{8,0},{12,4},{1,9},{5,13},{9,1},{13,5},{2,10},{6,14},... | collective-permute-start | bytes 589832 | tf_op jit(solution)/shard_map/ppermute | solution.py:481
  36.3 11.5 %collective-permute-start.14 = (bf16[2,1,64,768]{3,2,1,0:T(8,128)(2,1)S(1)}, bf16[2,1,64,768]{3,2,1,0:T(8,128)(2,1)S(1)}, u32[]{:S(2)}, u32[]{:S(2)}) collective-permute-start(bf16[2,1,64,768]{3,2,1,0:T(8,128)(2,1)S(1)} %get-tuple-element.41), channel_id=1, source_target_pairs={{8,1},{12,5},{1,8},{5,12},{9,2},{13,6},{2,9},{6,13},{10,3},{14,7},... | collective-permute-start | bytes 589832 | tf_op jit(solution)/shard_map/ppermute | solution.py:482
  38.5 10.6 %collective-permute-start.11 = (bf16[2,1,64,768]{3,2,1,0:T(8,128)(2,1)S(1)}, bf16[2,1,64,768]{3,2,1,0:T(8,128)(2,1)S(1)}, u32[]{:S(2)}, u32[]{:S(2)}) collective-permute-start(bf16[2,1,64,768]{3,2,1,0:T(8,128)(2,1)S(1)} %collective-permute-done.8.refs_0_.refs_2_), channel_id=1, source_target_pairs={{0,4},{4,0},{8,12},{12,8},{1,5},{5,1},{9,13},{13,9},{2,6},{6,2},{1... | collective-permute-start | bytes 589832 | tf_op jit(solution)/shard_map/ppermute | solution.py:450
  39.0 10.2 %collective-permute-start.12 = (bf16[2,1,64,768]{3,2,1,0:T(8,128)(2,1)S(1)}, bf16[2,1,64,768]{3,2,1,0:T(8,128)(2,1)S(1)}, u32[]{:S(2)}, u32[]{:S(2)}) collective-permute-start(bf16[2,1,64,768]{3,2,1,0:T(8,128)(2,1)S(1)} %collective-permute-done.9.refs_1_.refs_3_), channel_id=1, source_target_pairs={{0,4},{4,0},{8,12},{12,8},{1,5},{5,1},{9,13},{13,9},{2,6},{6,2},{1... | collective-permute-start | bytes 589832 | tf_op jit(solution)/shard_map/ppermute | solution.py:450
  47.0 2.1 %collective-permute-start.15 = (bf16[2,1,64,768]{3,2,1,0:T(8,128)(2,1)S(1)}, bf16[2,1,64,768]{3,2,1,0:T(8,128)(2,1)S(1)}, u32[]{:S(2)}, u32[]{:S(2)}) collective-permute-start(bf16[2,1,64,768]{3,2,1,0:T(8,128)(2,1)S(1)} %collective-permute-done.13.refs_6_), channel_id=1, source_target_pairs={{0,4},{4,0},{8,12},{12,8},{1,5},{5,1},{9,13},{13,9},{2,6},{6,2},{1... | collective-permute-start | bytes 589832 | tf_op jit(solution)/shard_map/ppermute | solution.py:450
  47.9 1.4 %collective-permute-start.16 = (bf16[2,1,64,768]{3,2,1,0:T(8,128)(2,1)S(1)}, bf16[2,1,64,768]{3,2,1,0:T(8,128)(2,1)S(1)}, u32[]{:S(2)}, u32[]{:S(2)}) collective-permute-start(bf16[2,1,64,768]{3,2,1,0:T(8,128)(2,1)S(1)} %collective-permute-done.14.refs_7_), channel_id=1, source_target_pairs={{0,4},{4,0},{8,12},{12,8},{1,5},{5,1},{9,13},{13,9},{2,6},{6,2},{1... | collective-permute-start | bytes 589832 | tf_op jit(solution)/shard_map/ppermute | solution.py:450
where the time goes:
time: 51.8 us; the launch traced here: 51.4 us
  starting transfers between devices  22.4 us (43%)
  Pallas kernels  13.2 us (25%)
  waiting for transfers between devices  12.7 us (25%)
  local copies, waits for them, and re-layouts  2.28 us (4%)
  between operations  0.83 us (2%)
    ppermute x5, starting transfers between devices, home(): return lax.ppermute(sent, axes, plan.member_perm(members - r))  8.71 us
    ppermute x2, waiting for transfers between devices, per_device(): nears.append(lax.ppermute(parts[0], axes, plan.frame_perm(0)))  8.47 us
    pallas_call x2, Pallas kernels, per_device(): pl.pallas_call(functools.partial(attend_kernel, plan, g), out_shape=[shap...  8.2 us
    ppermute x4, starting transfers between devices, per_device(): lax.ppermute(x, axes, plan.frame_perm(i))  6.66 us
    ppermute x2, starting transfers between devices, per_device(): fars.append(lax.ppermute(parts[1], axes, plan.frame_perm(1)))  4.11 us
    ppermute x4, waiting for transfers between devices, per_device(): lax.ppermute(x, axes, plan.frame_perm(i))  3.02 us
    unnamed x14, local copies, waits for them, and re-layouts  2.28 us
    pallas_call x1, Pallas kernels, per_device(): pl.pallas_call(functools.partial(add_kernel, plan), out_shape=[shape((row...  2.07 us
  transfers between devices with their start and end apart: 17, of which 6 were waited for; matrix products, arithmetic and copies ran while one was open for 0% of the time, Pallas kernels for 21%

commit v1 on v0

--- a/solution.py
+++ b/solution.py
@@ -367,7 +367,7 @@
                     start = (me + r) % members * plan.cols + plan.chunk_starts[g] * PAIR
                     total = pieces[r][2 + a, rows, columns].astype(jnp.float32)
                     for far, j, hit in hits:
-                        border = borders[(g * members + r) * 2 + far]
+                        border = borders[(g * members + r) * 2 + 1 - far]
                         total += jnp.where(hit, border[a, j].astype(jnp.float32), 0.0)
                     span = pl.ds(pl.multiple_of(start, PAIR), count * PAIR)
                     scratch[a, rows, span] = total.astype(jnp.bfloat16)
@@ -476,14 +476,14 @@
         parts = list(outs[members:])
         earlier += outs[:members]
         if g > 0:
-            held = hold(f"hold_far_{g}", [nears[-1], fars[-1]], parts[1], *earlier[1 - members :])
-            parts[1], earlier[1 - members :] = held[0], held[1:]
+            late = [parts[1], parts[0], *earlier[1 - members :]]
+            parts[1], parts[0], *earlier[1 - members :] = hold(f"hold_{g}", [fars[-1], nears[-1]], *late)
+        fars.append(lax.ppermute(parts[1], axes, plan.frame_perm(1)))
         nears.append(lax.ppermute(parts[0], axes, plan.frame_perm(0)))
-        fars.append(lax.ppermute(parts[1], axes, plan.frame_perm(1)))
     for near, far in zip(nears, fars, strict=True):
-        border_terms += [near, far]
+        border_terms += [far, near]
         for r in range(1, members):
-            border_terms += [home(near, r), home(far, r)]
+            border_terms += [home(far, r), home(near, r)]
     pieces = [earlier[-members], *[home(earlier[r - members], r) for r in range(1, members)]]
 
     attended, grad_queries = pl.pallas_call(

time: 51.8 us -> 55.2 us (1.066)
  the two profiles are of different devices: /device:TPU:21 before, /device:TPU:9 now
where the time goes in v1:
time: 55.2 us; the launch traced here: 54.7 us
  starting transfers between devices  29.7 us (54%)
  Pallas kernels  13 us (24%)
  waiting for transfers between devices  8.93 us (16%)
  local copies, waits for them, and re-layouts  2.28 us (4%)
  between operations  0.81 us (1%)
    ppermute x4, starting transfers between devices, per_device(): lax.ppermute(x, axes, plan.frame_perm(i))  10.9 us
    ppermute x5, starting transfers between devices, home(): return lax.ppermute(sent, axes, plan.member_perm(members - r))  9.36 us
    pallas_call x2, Pallas kernels, per_device(): pl.pallas_call(functools.partial(attend_kernel, plan, g), out_shape=[shap...  8.19 us
    ppermute x2, waiting for transfers between devices, per_device(): fars.append(lax.ppermute(parts[1], axes, plan.frame_perm(1)))  5.1 us
    ppermute x2, starting transfers between devices, per_device(): nears.append(lax.ppermute(parts[0], axes, plan.frame_perm(0)))  4.26 us
    ppermute x2, starting transfers between devices, per_device(): fars.append(lax.ppermute(parts[1], axes, plan.frame_perm(1)))  3.83 us
    ppermute x2, waiting for transfers between devices, per_device(): nears.append(lax.ppermute(parts[0], axes, plan.frame_perm(0)))  3.54 us
    unnamed x14, local copies, waits for them, and re-layouts  2.28 us
  transfers between devices with their start and end apart: 17, of which 4 were waited for; matrix products, arithmetic and copies ran while one was open for 0% of the time, Pallas kernels for 20%

profile of v1, /device:TPU:9, one launch (start us, length us, event | category | flops | bytes accessed | tf_op | source)
XLA Modules:
  0.0 54.7 jit_solution(399767338766061031)
XLA Ops:
  0.6 0.0 copy-start
  0.6 0.0 copy-start.1
  0.7 0.7 %collective-permute-start = (bf16[128,3072]{1,0:T(8,128)(2,1)}, bf16[128,3072]{1,0:T(8,128)(2,1)S(1)}, u32[]{:S(2)}, u32[]{:S(2)}) collective-permute-start(bf16[128,3072]{1,0:T(8,128)(2,1)} %refs_1_.9), channel_id=1, source_target_pairs={{0,4},{4,0},{8,12},{12,8},{1,5},{5,1},{9,13},{13,9},{2,6},{6,2},{1... | collective-permute-start | bytes 2359304 | tf_op jit(solution)/shard_map/ppermute | solution.py:396
  1.4 0.1 collective-permute-start.1
  1.5 1.1 %copy-done.2 = bf16[128,3072]{1,0:T(8,128)(2,1)S(1)} copy-done((bf16[128,3072]{1,0:T(8,128)(2,1)S(1)}, bf16[128,3072]{1,0:T(8,128)(2,1)}, u32[]{:S(2)}) %copy-start.2) | copy-done | bytes 786456
  2.6 1.1 %copy-done.4 = bf16[128,3072]{1,0:T(8,128)(2,1)S(1)} copy-done((bf16[128,3072]{1,0:T(8,128)(2,1)S(1)}, bf16[128,3072]{1,0:T(8,128)(2,1)}, u32[]{:S(2)}) %copy-start.4) | copy-done | bytes 786456
  3.7 0.1 split_qg.1
  3.8 0.5 collective-permute-start.2
  4.3 0.1 collective-permute-start.3
  4.4 0.0 collective-permute-done.refs_2_.refs_4_
  4.4 0.3 collective-permute-done.1.refs_3_.refs_5_
  4.6 0.0 copy-done
  4.6 0.0 copy-done.1
  4.7 0.7 %pick_0.1 = (bf16[2,1,64,768]{3,2,1,0:T(8,128)(2,1)S(1)}, bf16[2,1,64,768]{3,2,1,0:T(8,128)(2,1)S(1)}) custom-call(s32[3,32]{1,0:T(4,128)S(1)} %bitcast.1, s32[32]{0:T(128)S(1)} %copy-done.6, bf16[128,3072]{1,0:T(8,128)(2,1)S(1)} %copy-done, bf16[128,3072]{1,0:T(8,128)(2,1)S(1)} %copy-done.1, bf16[128,3072]{1,0:T(8,128)(2,1)S(1)} %collective-permute-done.refs_2_.refs_4_, ...), custom_call_target="tpu_custom_call" | custom-call | bytes 786432 | tf_op jit(solution)/shard_map/pick_0/pallas_call | solution.py:434
  5.4 1.3 %collective-permute-start.4 = (bf16[2,1,64,768]{3,2,1,0:T(8,128)(2,1)S(1)}, bf16[2,1,64,768]{3,2,1,0:T(8,128)(2,1)S(1)}, u32[]{:S(2)}, u32[]{:S(2)}) collective-permute-start(bf16[2,1,64,768]{3,2,1,0:T(8,128)(2,1)S(1)} %get-tuple-element.27), channel_id=1, source_target_pairs={{0,8},{4,12},{8,0},{12,4},{1,9},{5,13},{9,1},{13,5},{2,10},{6,14},... | collective-permute-start | bytes 589832 | tf_op jit(solution)/shard_map/ppermute | solution.py:446
  6.7 2.0 %collective-permute-start.7 = (bf16[2,1,64,768]{3,2,1,0:T(8,128)(2,1)S(1)}, bf16[2,1,64,768]{3,2,1,0:T(8,128)(2,1)S(1)}, u32[]{:S(2)}, u32[]{:S(2)}) collective-permute-start(bf16[2,1,64,768]{3,2,1,0:T(8,128)(2,1)S(1)} %get-tuple-element.30), channel_id=1, source_target_pairs={{8,1},{12,5},{1,8},{5,12},{9,2},{13,6},{2,9},{6,13},{10,3},{14,7},... | collective-permute-start | bytes 589832 | tf_op jit(solution)/shard_map/ppermute | solution.py:446
  8.8 0.7 %pick_1.1 = (bf16[2,1,64,768]{3,2,1,0:T(8,128)(2,1)S(1)}, bf16[2,1,64,768]{3,2,1,0:T(8,128)(2,1)S(1)}) custom-call(s32[3,32]{1,0:T(4,128)S(1)} %bitcast.2, s32[32]{0:T(128)S(1)} %copy-done.6, bf16[128,3072]{1,0:T(8,128)(2,1)S(1)} %copy-done, bf16[128,3072]{1,0:T(8,128)(2,1)S(1)} %copy-done.1, bf16[128,3072]{1,0:T(8,128)(2,1)S(1)} %collective-permute-done.refs_2_.refs_4_, ...), custom_call_target="tpu_custom_call" | custom-call | bytes 786432 | tf_op jit(solution)/shard_map/pick_1/pallas_call | solution.py:434
  9.5 4.3 %collective-permute-start.6 = (bf16[2,1,64,768]{3,2,1,0:T(8,128)(2,1)S(1)}, bf16[2,1,64,768]{3,2,1,0:T(8,128)(2,1)S(1)}, u32[]{:S(2)}, u32[]{:S(2)}) collective-permute-start(bf16[2,1,64,768]{3,2,1,0:T(8,128)(2,1)S(1)} %get-tuple-element.29), channel_id=1, source_target_pairs={{8,1},{12,5},{1,8},{5,12},{9,2},{13,6},{2,9},{6,13},{10,3},{14,7},... | collective-permute-start | bytes 589832 | tf_op jit(solution)/shard_map/ppermute | solution.py:446
  13.8 0.0 collective-permute-done.4.refs_0_.refs_8_
  13.8 3.3 %collective-permute-start.5 = (bf16[2,1,64,768]{3,2,1,0:T(8,128)(2,1)S(1)}, bf16[2,1,64,768]{3,2,1,0:T(8,128)(2,1)S(1)}, u32[]{:S(2)}, u32[]{:S(2)}) collective-permute-start(bf16[2,1,64,768]{3,2,1,0:T(8,128)(2,1)S(1)} %hold_near_1.1), channel_id=1, source_target_pairs={{0,8},{4,12},{8,0},{12,4},{1,9},{5,13},{9,1},{13,5},{2,10},{6,14},... | collective-permute-start | bytes 589832 | tf_op jit(solution)/shard_map/ppermute | solution.py:446
  17.1 0.0 collective-permute-done.2.refs_6_
  17.1 0.0 collective-permute-done.3.refs_7_
  17.1 0.0 collective-permute-done.7.refs_9_
  17.1 4.1 %attend_0.1 = (bf16[4,128,768]{2,1,0:T(8,128)(2,1)S(1)}, bf16[4,128,768]{2,1,0:T(8,128)(2,1)S(1)}, bf16[2,1,64,768]{3,2,1,0:T(8,128)(2,1)S(1)}, bf16[2,1,64,768]{3,2,1,0:T(8,128)(2,1)S(1)}) custom-call(s32[3,32]{1,0:T(4,128)S(1)} %bitcast.3, s32[32]{0:T(128)S(1)} %copy-done.6, bf16[128,3072]{1,0:T(8,128)(2,1)S(1)} %copy-done.3, ...), custom_call_target="tpu_custom_call" | custom-call | flops 905969664 | bytes 3145728 | tf_op jit(solution)/shard_map/attend_0/pallas_call | solution.py:457
  21.2 1.9 %collective-permute-start.8 = (bf16[2,1,64,768]{3,2,1,0:T(8,128)(2,1)S(1)}, bf16[2,1,64,768]{3,2,1,0:T(8,128)(2,1)S(1)}, u32[]{:S(2)}, u32[]{:S(2)}) collective-permute-start(bf16[2,1,64,768]{3,2,1,0:T(8,128)(2,1)S(1)} %get-tuple-element.34), channel_id=1, source_target_pairs={{8,1},{12,5},{1,8},{5,12},{9,2},{13,6},{2,9},{6,13},{10,3},{14,7},... | collective-permute-start | bytes 589832 | tf_op jit(solution)/shard_map/ppermute | solution.py:481
  23.1 2.5 %collective-permute-start.9 = (bf16[2,1,64,768]{3,2,1,0:T(8,128)(2,1)S(1)}, bf16[2,1,64,768]{3,2,1,0:T(8,128)(2,1)S(1)}, u32[]{:S(2)}, u32[]{:S(2)}) collective-permute-start(bf16[2,1,64,768]{3,2,1,0:T(8,128)(2,1)S(1)} %get-tuple-element.35), channel_id=1, source_target_pairs={{0,8},{4,12},{8,0},{12,4},{1,9},{5,13},{9,1},{13,5},{2,10},{6,14},... | collective-permute-start | bytes 589832 | tf_op jit(solution)/shard_map/ppermute | solution.py:482
  25.7 0.0 collective-permute-done.6.refs_9_
  25.7 0.0 collective-permute-done.5.refs_8_
  25.7 4.1 %attend_1.1 = (bf16[4,128,1536]{2,1,0:T(8,128)(2,1)S(1)}, bf16[4,128,1536]{2,1,0:T(8,128)(2,1)S(1)}, bf16[2,1,64,768]{3,2,1,0:T(8,128)(2,1)S(1)}, bf16[2,1,64,768]{3,2,1,0:T(8,128)(2,1)S(1)}) custom-call(s32[3,32]{1,0:T(4,128)S(1)} %bitcast.4, s32[32]{0:T(128)S(1)} %copy-done.6, bf16[128,3072]{1,0:T(8,128)(2,1)S(1)} %copy-done.3, ...), custom_call_target="tpu_custom_call" | custom-call | flops 905969664 | bytes 3145728 | tf_op jit(solution)/shard_map/attend_1/pallas_call | solution.py:457
  29.8 0.0 collective-permute-done.8.refs_0_.refs_2_
  29.8 0.8 %collective-permute-done.9.refs_1_.refs_3_ = bf16[2,1,64,768]{3,2,1,0:T(8,128)(2,1)S(1)} collective-permute-done((bf16[2,1,64,768]{3,2,1,0:T(8,128)(2,1)S(1)}, bf16[2,1,64,768]{3,2,1,0:T(8,128)(2,1)S(1)}, u32[]{:S(2)}, u32[]{:S(2)}) %collective-permute-start.9) | collective-permute-done | bytes 196640 | tf_op jit(solution)/shard_map/ppermute | solution.py:482
  30.6 0.1 hold_1.1
  30.8 7.1 %collective-permute-start.10 = (bf16[4,128,1536]{2,1,0:T(8,128)(2,1)S(1)}, bf16[4,128,1536]{2,1,0:T(8,128)(2,1)S(1)}, u32[]{:S(2)}, u32[]{:S(2)}) collective-permute-start(bf16[4,128,1536]{2,1,0:T(8,128)(2,1)S(1)} %get-tuple-element.39), channel_id=1, source_target_pairs={{0,4},{4,0},{8,12},{12,8},{1,5},{5,1},{9,13},{13,9},{2,6},{6,2},{1... | collective-permute-start | bytes 4718600 | tf_op jit(solution)/shard_map/ppermute | solution.py:450
  37.9 1.9 %collective-permute-start.13 = (bf16[2,1,64,768]{3,2,1,0:T(8,128)(2,1)S(1)}, bf16[2,1,64,768]{3,2,1,0:T(8,128)(2,1)S(1)}, u32[]{:S(2)}, u32[]{:S(2)}) collective-permute-start(bf16[2,1,64,768]{3,2,1,0:T(8,128)(2,1)S(1)} %get-tuple-element.42), channel_id=1, source_target_pairs={{8,1},{12,5},{1,8},{5,12},{9,2},{13,6},{2,9},{6,13},{10,3},{14,7},... | collective-permute-start | bytes 589832 | tf_op jit(solution)/shard_map/ppermute | solution.py:481
  39.8 1.7 %collective-permute-start.14 = (bf16[2,1,64,768]{3,2,1,0:T(8,128)(2,1)S(1)}, bf16[2,1,64,768]{3,2,1,0:T(8,128)(2,1)S(1)}, u32[]{:S(2)}, u32[]{:S(2)}) collective-permute-start(bf16[2,1,64,768]{3,2,1,0:T(8,128)(2,1)S(1)} %get-tuple-element.43), channel_id=1, source_target_pairs={{0,8},{4,12},{8,0},{12,4},{1,9},{5,13},{9,1},{13,5},{2,10},{6,14},... | collective-permute-start | bytes 589832 | tf_op jit(solution)/shard_map/ppermute | solution.py:482
  41.5 0.6 %collective-permute-start.11 = (bf16[2,1,64,768]{3,2,1,0:T(8,128)(2,1)S(1)}, bf16[2,1,64,768]{3,2,1,0:T(8,128)(2,1)S(1)}, u32[]{:S(2)}, u32[]{:S(2)}) collective-permute-start(bf16[2,1,64,768]{3,2,1,0:T(8,128)(2,1)S(1)} %collective-permute-done.8.refs_0_.refs_2_), channel_id=1, source_target_pairs={{0,4},{4,0},{8,12},{12,8},{1,5},{5,1},{9,13},{13,9},{2,6},{6,2},{1... | collective-permute-start | bytes 589832 | tf_op jit(solution)/shard_map/ppermute | solution.py:450
  42.1 0.0 collective-permute-start.12
  42.1 5.1 %collective-permute-done.13.refs_6_ = bf16[2,1,64,768]{3,2,1,0:T(8,128)(2,1)S(1)} collective-permute-done((bf16[2,1,64,768]{3,2,1,0:T(8,128)(2,1)S(1)}, bf16[2,1,64,768]{3,2,1,0:T(8,128)(2,1)S(1)}, u32[]{:S(2)}, u32[]{:S(2)}) %collective-permute-start.13) | collective-permute-done | bytes 196640 | tf_op jit(solution)/shard_map/ppermute | solution.py:481
  47.2 0.9 %collective-permute-start.15 = (bf16[2,1,64,768]{3,2,1,0:T(8,128)(2,1)S(1)}, bf16[2,1,64,768]{3,2,1,0:T(8,128)(2,1)S(1)}, u32[]{:S(2)}, u32[]{:S(2)}) collective-permute-start(bf16[2,1,64,768]{3,2,1,0:T(8,128)(2,1)S(1)} %collective-permute-done.13.refs_6_), channel_id=1, source_target_pairs={{0,4},{4,0},{8,12},{12,8},{1,5},{5,1},{9,13},{13,9},{2,6},{6,2},{1... | collective-permute-start | bytes 589832 | tf_op jit(solution)/shard_map/ppermute | solution.py:450
  48.1 2.7 %collective-permute-done.14.refs_7_ = bf16[2,1,64,768]{3,2,1,0:T(8,128)(2,1)S(1)} collective-permute-done((bf16[2,1,64,768]{3,2,1,0:T(8,128)(2,1)S(1)}, bf16[2,1,64,768]{3,2,1,0:T(8,128)(2,1)S(1)}, u32[]{:S(2)}, u32[]{:S(2)}) %collective-permute-start.14) | collective-permute-done | bytes 196640 | tf_op jit(solution)/shard_map/ppermute | solution.py:482
  50.8 0.8 %collective-permute-start.16 = (bf16[2,1,64,768]{3,2,1,0:T(8,128)(2,1)S(1)}, bf16[2,1,64,768]{3,2,1,0:T(8,128)(2,1)S(1)}, u32[]{:S(2)}, u32[]{:S(2)}) collective-permute-start(bf16[2,1,64,768]{3,2,1,0:T(8,128)(2,1)S(1)} %collective-permute-done.14.refs_7_), channel_id=1, source_target_pairs={{0,4},{4,0},{8,12},{12,8},{1,5},{5,1},{9,13},{13,9},{2,6},{6,2},{1... | collective-permute-start | bytes 589832 | tf_op jit(solution)/shard_map/ppermute | solution.py:450
  51.6 0.0 collective-permute-done.10.refs_1_
  51.6 1.2 %join.1 = (bf16[128,3072]{1,0:T(8,128)(2,1)}, bf16[128,3072]{1,0:T(8,128)(2,1)}) custom-call(bf16[4,128,1536]{2,1,0:T(8,128)(2,1)S(1)} %get-tuple-element.33.refs_0_, bf16[4,128,1536]{2,1,0:T(8,128)(2,1)S(1)} %collective-permute-done.10.refs_1_), custom_call_target="tpu_custom_call" | custom-call | bytes 3145728 | tf_op jit(solution)/shard_map/join/pallas_call | solution.py:489
  52.8 0.0 collective-permute-done.11.refs_4_
  52.8 0.0 collective-permute-done.12.refs_5_
  52.8 0.0 collective-permute-done.15.refs_8_
  52.8 0.0 collective-permute-done.16.refs_9_
  52.9 1.9 %add.1 = (bf16[128,3072]{1,0:T(8,128)(2,1)}, bf16[128,3072]{1,0:T(8,128)(2,1)}) custom-call(s32[3,32]{1,0:T(4,128)S(1)} %bitcast.5, s32[32]{0:T(128)S(1)} %copy-done.6, bf16[4,128,1536]{2,1,0:T(8,128)(2,1)S(1)} %get-tuple-element.33.refs_0_, bf16[4,128,1536]{2,1,0:T(8,128)(2,1)S(1)} %collective-permute-done.10.refs_1_, ...), custom_call_target="tpu_custom_call" | custom-call | bytes 3932160 | tf_op jit(solution)/shard_map/add/pallas_call | solution.py:499
  (9 shorter events, 0.0 us)
Async XLA Ops:
  0.6 4.0 %copy-start = (bf16[128,3072]{1,0:T(8,128)(2,1)S(1)}, bf16[128,3072]{1,0:T(8,128)(2,1)}, u32[]{:S(2)}) copy-start(bf16[128,3072]{1,0:T(8,128)(2,1)} %refs_1_.9) | copy-start | bytes 2359300
  0.6 4.0 %copy-start.1 = (bf16[128,3072]{1,0:T(8,128)(2,1)S(1)}, bf16[128,3072]{1,0:T(8,128)(2,1)}, u32[]{:S(2)}) copy-start(bf16[128,3072]{1,0:T(8,128)(2,1)} %refs_2_.3) | copy-start | bytes 2359300
  0.7 3.7 %collective-permute-start = (bf16[128,3072]{1,0:T(8,128)(2,1)}, bf16[128,3072]{1,0:T(8,128)(2,1)S(1)}, u32[]{:S(2)}, u32[]{:S(2)}) collective-permute-start(bf16[128,3072]{1,0:T(8,128)(2,1)} %refs_1_.9), channel_id=1, source_target_pairs={{0,4},{4,0},{8,12},{12,8},{1,5},{5,1},{9,13},{13,9},{2,6},{6,2},{1... | collective-permute-start | bytes 2359304 | tf_op jit(solution)/shard_map/ppermute | solution.py:396
  1.4 3.2 %collective-permute-start.1 = (bf16[128,3072]{1,0:T(8,128)(2,1)}, bf16[128,3072]{1,0:T(8,128)(2,1)S(1)}, u32[]{:S(2)}, u32[]{:S(2)}) collective-permute-start(bf16[128,3072]{1,0:T(8,128)(2,1)} %refs_2_.3), channel_id=1, source_target_pairs={{0,4},{4,0},{8,12},{12,8},{1,5},{5,1},{9,13},{13,9},{2,6},{6,2},{1... | collective-permute-start | bytes 2359304 | tf_op jit(solution)/shard_map/ppermute | solution.py:396
  1.5 1.1 %copy-start.2 = (bf16[128,3072]{1,0:T(8,128)(2,1)S(1)}, bf16[128,3072]{1,0:T(8,128)(2,1)}, u32[]{:S(2)}) copy-start(bf16[128,3072]{1,0:T(8,128)(2,1)} %refs_0_.9) | copy-start | bytes 2359300
  2.6 1.1 %copy-start.4 = (bf16[128,3072]{1,0:T(8,128)(2,1)S(1)}, bf16[128,3072]{1,0:T(8,128)(2,1)}, u32[]{:S(2)}) copy-start(bf16[128,3072]{1,0:T(8,128)(2,1)} %refs_3_.3) | copy-start | bytes 2359300
  3.7 0.9 %copy-start.5 = (s32[32,3]{0,1:T(4,128)S(1)}, s32[32,3]{0,1:T(4,128)}, u32[]{:S(2)}) copy-start(s32[32,3]{0,1:T(4,128)} %param.10) | copy-start | bytes 1156
  3.7 0.9 %copy-start.6 = (s32[32]{0:T(128)S(1)}, s32[32]{0:T(128)}, u32[]{:S(2)}) copy-start(s32[32]{0:T(128)} %counts_ref.9) | copy-start | bytes 388
  3.8 13.3 %collective-permute-start.2 = (bf16[128,1536]{1,0:T(8,128)(2,1)S(1)}, bf16[128,1536]{1,0:T(8,128)(2,1)S(1)}, u32[]{:S(2)}, u32[]{:S(2)}) collective-permute-start(bf16[128,1536]{1,0:T(8,128)(2,1)S(1)} %get-tuple-element.25), channel_id=1, source_target_pairs={{0,4},{4,0},{8,12},{12,8},{1,5},{5,1},{9,13},{13,9},{2,6},{6,2},{1... | collective-permute-start | bytes 1179656 | tf_op jit(solution)/shard_map/ppermute | solution.py:412
  4.3 12.8 %collective-permute-start.3 = (bf16[128,1536]{1,0:T(8,128)(2,1)S(1)}, bf16[128,1536]{1,0:T(8,128)(2,1)S(1)}, u32[]{:S(2)}, u32[]{:S(2)}) collective-permute-start(bf16[128,1536]{1,0:T(8,128)(2,1)S(1)} %get-tuple-element.26), channel_id=1, source_target_pairs={{0,4},{4,0},{8,12},{12,8},{1,5},{5,1},{9,13},{13,9},{2,6},{6,2},{1... | collective-permute-start | bytes 1179656 | tf_op jit(solution)/shard_map/ppermute | solution.py:412
  5.4 8.4 %collective-permute-start.4 = (bf16[2,1,64,768]{3,2,1,0:T(8,128)(2,1)S(1)}, bf16[2,1,64,768]{3,2,1,0:T(8,128)(2,1)S(1)}, u32[]{:S(2)}, u32[]{:S(2)}) collective-permute-start(bf16[2,1,64,768]{3,2,1,0:T(8,128)(2,1)S(1)} %get-tuple-element.27), channel_id=1, source_target_pairs={{0,8},{4,12},{8,0},{12,4},{1,9},{5,13},{9,1},{13,5},{2,10},{6,14},... | collective-permute-start | bytes 589832 | tf_op jit(solution)/shard_map/ppermute | solution.py:446
  6.7 10.4 %copy-start.3 = (bf16[128,3072]{1,0:T(8,128)(2,1)S(1)}, bf16[128,3072]{1,0:T(8,128)(2,1)}, u32[]{:S(2)}) copy-start(bf16[128,3072]{1,0:T(8,128)(2,1)} %refs_0_.9) | copy-start | bytes 2359300
  6.7 10.4 %collective-permute-start.7 = (bf16[2,1,64,768]{3,2,1,0:T(8,128)(2,1)S(1)}, bf16[2,1,64,768]{3,2,1,0:T(8,128)(2,1)S(1)}, u32[]{:S(2)}, u32[]{:S(2)}) collective-permute-start(bf16[2,1,64,768]{3,2,1,0:T(8,128)(2,1)S(1)} %get-tuple-element.30), channel_id=1, source_target_pairs={{8,1},{12,5},{1,8},{5,12},{9,2},{13,6},{2,9},{6,13},{10,3},{14,7},... | collective-permute-start | bytes 589832 | tf_op jit(solution)/shard_map/ppermute | solution.py:446
  9.5 16.1 %collective-permute-start.6 = (bf16[2,1,64,768]{3,2,1,0:T(8,128)(2,1)S(1)}, bf16[2,1,64,768]{3,2,1,0:T(8,128)(2,1)S(1)}, u32[]{:S(2)}, u32[]{:S(2)}) collective-permute-start(bf16[2,1,64,768]{3,2,1,0:T(8,128)(2,1)S(1)} %get-tuple-element.29), channel_id=1, source_target_pairs={{8,1},{12,5},{1,8},{5,12},{9,2},{13,6},{2,9},{6,13},{10,3},{14,7},... | collective-permute-start | bytes 589832 | tf_op jit(solution)/shard_map/ppermute | solution.py:446
  13.8 11.8 %collective-permute-start.5 = (bf16[2,1,64,768]{3,2,1,0:T(8,128)(2,1)S(1)}, bf16[2,1,64,768]{3,2,1,0:T(8,128)(2,1)S(1)}, u32[]{:S(2)}, u32[]{:S(2)}) collective-permute-start(bf16[2,1,64,768]{3,2,1,0:T(8,128)(2,1)S(1)} %hold_near_1.1), channel_id=1, source_target_pairs={{0,8},{4,12},{8,0},{12,4},{1,9},{5,13},{9,1},{13,5},{2,10},{6,14},... | collective-permute-start | bytes 589832 | tf_op jit(solution)/shard_map/ppermute | solution.py:446
  21.2 8.6 %collective-permute-start.8 = (bf16[2,1,64,768]{3,2,1,0:T(8,128)(2,1)S(1)}, bf16[2,1,64,768]{3,2,1,0:T(8,128)(2,1)S(1)}, u32[]{:S(2)}, u32[]{:S(2)}) collective-permute-start(bf16[2,1,64,768]{3,2,1,0:T(8,128)(2,1)S(1)} %get-tuple-element.34), channel_id=1, source_target_pairs={{8,1},{12,5},{1,8},{5,12},{9,2},{13,6},{2,9},{6,13},{10,3},{14,7},... | collective-permute-start | bytes 589832 | tf_op jit(solution)/shard_map/ppermute | solution.py:481
  23.1 7.5 %collective-permute-start.9 = (bf16[2,1,64,768]{3,2,1,0:T(8,128)(2,1)S(1)}, bf16[2,1,64,768]{3,2,1,0:T(8,128)(2,1)S(1)}, u32[]{:S(2)}, u32[]{:S(2)}) collective-permute-start(bf16[2,1,64,768]{3,2,1,0:T(8,128)(2,1)S(1)} %get-tuple-element.35), channel_id=1, source_target_pairs={{0,8},{4,12},{8,0},{12,4},{1,9},{5,13},{9,1},{13,5},{2,10},{6,14},... | collective-permute-start | bytes 589832 | tf_op jit(solution)/shard_map/ppermute | solution.py:482
  30.8 20.8 %collective-permute-start.10 = (bf16[4,128,1536]{2,1,0:T(8,128)(2,1)S(1)}, bf16[4,128,1536]{2,1,0:T(8,128)(2,1)S(1)}, u32[]{:S(2)}, u32[]{:S(2)}) collective-permute-start(bf16[4,128,1536]{2,1,0:T(8,128)(2,1)S(1)} %get-tuple-element.39), channel_id=1, source_target_pairs={{0,4},{4,0},{8,12},{12,8},{1,5},{5,1},{9,13},{13,9},{2,6},{6,2},{1... | collective-permute-start | bytes 4718600 | tf_op jit(solution)/shard_map/ppermute | solution.py:450
  37.9 9.3 %collective-permute-start.13 = (bf16[2,1,64,768]{3,2,1,0:T(8,128)(2,1)S(1)}, bf16[2,1,64,768]{3,2,1,0:T(8,128)(2,1)S(1)}, u32[]{:S(2)}, u32[]{:S(2)}) collective-permute-start(bf16[2,1,64,768]{3,2,1,0:T(8,128)(2,1)S(1)} %get-tuple-element.42), channel_id=1, source_target_pairs={{8,1},{12,5},{1,8},{5,12},{9,2},{13,6},{2,9},{6,13},{10,3},{14,7},... | collective-permute-start | bytes 589832 | tf_op jit(solution)/shard_map/ppermute | solution.py:481
  39.8 11.0 %collective-permute-start.14 = (bf16[2,1,64,768]{3,2,1,0:T(8,128)(2,1)S(1)}, bf16[2,1,64,768]{3,2,1,0:T(8,128)(2,1)S(1)}, u32[]{:S(2)}, u32[]{:S(2)}) collective-permute-start(bf16[2,1,64,768]{3,2,1,0:T(8,128)(2,1)S(1)} %get-tuple-element.43), channel_id=1, source_target_pairs={{0,8},{4,12},{8,0},{12,4},{1,9},{5,13},{9,1},{13,5},{2,10},{6,14},... | collective-permute-start | bytes 589832 | tf_op jit(solution)/shard_map/ppermute | solution.py:482
  41.5 11.3 %collective-permute-start.11 = (bf16[2,1,64,768]{3,2,1,0:T(8,128)(2,1)S(1)}, bf16[2,1,64,768]{3,2,1,0:T(8,128)(2,1)S(1)}, u32[]{:S(2)}, u32[]{:S(2)}) collective-permute-start(bf16[2,1,64,768]{3,2,1,0:T(8,128)(2,1)S(1)} %collective-permute-done.8.refs_0_.refs_2_), channel_id=1, source_target_pairs={{0,4},{4,0},{8,12},{12,8},{1,5},{5,1},{9,13},{13,9},{2,6},{6,2},{1... | collective-permute-start | bytes 589832 | tf_op jit(solution)/shard_map/ppermute | solution.py:450
  42.1 10.7 %collective-permute-start.12 = (bf16[2,1,64,768]{3,2,1,0:T(8,128)(2,1)S(1)}, bf16[2,1,64,768]{3,2,1,0:T(8,128)(2,1)S(1)}, u32[]{:S(2)}, u32[]{:S(2)}) collective-permute-start(bf16[2,1,64,768]{3,2,1,0:T(8,128)(2,1)S(1)} %collective-permute-done.9.refs_1_.refs_3_), channel_id=1, source_target_pairs={{0,4},{4,0},{8,12},{12,8},{1,5},{5,1},{9,13},{13,9},{2,6},{6,2},{1... | collective-permute-start | bytes 589832 | tf_op jit(solution)/shard_map/ppermute | solution.py:450
  47.2 5.6 %collective-permute-start.15 = (bf16[2,1,64,768]{3,2,1,0:T(8,128)(2,1)S(1)}, bf16[2,1,64,768]{3,2,1,0:T(8,128)(2,1)S(1)}, u32[]{:S(2)}, u32[]{:S(2)}) collective-permute-start(bf16[2,1,64,768]{3,2,1,0:T(8,128)(2,1)S(1)} %collective-permute-done.13.refs_6_), channel_id=1, source_target_pairs={{0,4},{4,0},{8,12},{12,8},{1,5},{5,1},{9,13},{13,9},{2,6},{6,2},{1... | collective-permute-start | bytes 589832 | tf_op jit(solution)/shard_map/ppermute | solution.py:450
  50.8 2.1 %collective-permute-start.16 = (bf16[2,1,64,768]{3,2,1,0:T(8,128)(2,1)S(1)}, bf16[2,1,64,768]{3,2,1,0:T(8,128)(2,1)S(1)}, u32[]{:S(2)}, u32[]{:S(2)}) collective-permute-start(bf16[2,1,64,768]{3,2,1,0:T(8,128)(2,1)S(1)} %collective-permute-done.14.refs_7_), channel_id=1, source_target_pairs={{0,4},{4,0},{8,12},{12,8},{1,5},{5,1},{9,13},{13,9},{2,6},{6,2},{1... | collective-permute-start | bytes 589832 | tf_op jit(solution)/shard_map/ppermute | solution.py:450

commit v2 on v0

--- a/solution.py
+++ b/solution.py
@@ -342,37 +342,78 @@
     write_out(scratch, outs, sem, fill)
 
 
+def touching(plan, lists_ref, counts_ref):
+    frame, me = position(plan)
+    partners = [partner(frame, far) for far in range(2)]
+    picks = [listed(plan, lists_ref, counts_ref, other, frame) for other in partners]
+
+    def hits(i):
+        found = []
+        for far in range(2):
+            exists = (partners[far] >= 0) & (partners[far] < plan.frames)
+            for j, pick in enumerate(picks[far]):
+                found.append((far, j, exists & (pick == me * plan.device_tiles + i)))
+        return found, functools.reduce(lambda x, y: x | y, [hit for _, _, hit in found])
+
+    return me, hits
+
+
+def summed(plan, g, a, rows, piece, borders, found):
+    columns = pl.ds(plan.chunk_starts[g] * PAIR, plan.chunk_pairs[g] * PAIR)
+    total = piece[2 + a, rows, columns].astype(jnp.float32)
+    for far, j, hit in found:
+        total += jnp.where(hit, borders[far][a, j].astype(jnp.float32), 0.0)
+    return total.astype(jnp.bfloat16)
+
+
 def add_kernel(plan, lists_ref, counts_ref, *refs):
     members, outs, scratch, sem = plan.members, refs[-4:-2], refs[-2], refs[-1]
     pieces, borders = refs[:members], refs[members:-4]
-    frame, me = position(plan)
-    partners = [partner(frame, far) for far in range(2)]
-    picks = [listed(plan, lists_ref, counts_ref, other, frame) for other in partners]
+    me, hits = touching(plan, lists_ref, counts_ref)
 
     def fill(a, i, rows):
-        hits = []
-        for far in range(2):
-            exists = (partners[far] >= 0) & (partners[far] < plan.frames)
-            for j, pick in enumerate(picks[far]):
-                hits.append((far, j, exists & (pick == me * plan.device_tiles + i)))
+        found, touched = hits(i)
         for r in range(members):
             start = pl.multiple_of((me + r) % members * plan.cols, PAIR)
             scratch[a, rows, pl.ds(start, plan.cols)] = pieces[r][2 + a, rows, :]
 
-        @pl.when(functools.reduce(lambda x, y: x | y, [hit for _, _, hit in hits]))
+        @pl.when(touched)
         def _():
-            for g, count in enumerate(plan.chunk_pairs):
-                for r in range(members):
-                    columns = pl.ds(plan.chunk_starts[g] * PAIR, count * PAIR)
-                    start = (me + r) % members * plan.cols + plan.chunk_starts[g] * PAIR
-                    total = pieces[r][2 + a, rows, columns].astype(jnp.float32)
-                    for far, j, hit in hits:
-                        border = borders[(g * members + r) * 2 + far]
-                        total += jnp.where(hit, border[a, j].astype(jnp.float32), 0.0)
-                    span = pl.ds(pl.multiple_of(start, PAIR), count * PAIR)
-                    scratch[a, rows, span] = total.astype(jnp.bfloat16)
+            for r in range(members):
+                span = pl.ds(pl.multiple_of((me + r) % members * plan.cols, PAIR), plan.chunk_pairs[0] * PAIR)
+                scratch[a, rows, span] = summed(plan, 0, a, rows, pieces[r], borders[2 * r : 2 * r + 2], found)
 
     write_out(scratch, outs, sem, fill)
+
+
+def patch_kernel(plan, lists_ref, counts_ref, *refs):
+    members, outs, scratch, sem = plan.members, refs[-4:-2], refs[-2], refs[-1]
+    pieces, borders = refs[:members], refs[members : 3 * members]
+    me, hits = touching(plan, lists_ref, counts_ref)
+    cols = plan.chunk_pairs[1] * PAIR
+
+    def copy(a, i, r):
+        start = (me + r) % members * plan.cols + plan.chunk_starts[1] * PAIR
+        target = outs[a].at[pl.ds(i * TILE, TILE), pl.ds(pl.multiple_of(start, PAIR), cols)]
+        slot = (a * plan.device_tiles + i) * members + r
+        return pltpu.make_async_copy(scratch.at[slot], target, sem.at[slot])
+
+    places = [(a, i, r) for i in range(plan.device_tiles) for a in range(2) for r in range(members)]
+    for a, i, r in places:
+        found, touched = hits(i)
+
+        @pl.when(touched)
+        def _():
+            rows = pl.ds(i * TILE, TILE)
+            slot = (a * plan.device_tiles + i) * members + r
+            scratch[slot] = summed(plan, 1, a, rows, pieces[r], borders[2 * r : 2 * r + 2], found)
+            copy(a, i, r).start()
+
+    for a, i, r in places:
+
+        @pl.when(hits(i)[1])
+        def _():
+            copy(a, i, r).wait()
 
 
 def per_device(queries, key_vectors, value_vectors, grad_out, key_tiles, tile_counts):
@@ -449,7 +490,7 @@
     def home(sent, r):
         return lax.ppermute(sent, axes, plan.member_perm(members - r))
 
-    earlier, border_terms, nears, fars = [], [], [], []
+    earlier, nears, fars = [], [], []
     for g, count in enumerate(plan.chunk_pairs):
         cols = count * PAIR
         wide = plan.cols if g == chunks - 1 else cols
@@ -480,10 +521,9 @@
             parts[1], earlier[1 - members :] = held[0], held[1:]
         nears.append(lax.ppermute(parts[0], axes, plan.frame_perm(0)))
         fars.append(lax.ppermute(parts[1], axes, plan.frame_perm(1)))
-    for near, far in zip(nears, fars, strict=True):
-        border_terms += [near, far]
-        for r in range(1, members):
-            border_terms += [home(near, r), home(far, r)]
+    def everyone(near, far):
+        return [near, far] + [home(x, r) for r in range(1, members) for x in (near, far)]
+
     pieces = [earlier[-members], *[home(earlier[r - members], r) for r in range(1, members)]]
 
     attended, grad_queries = pl.pallas_call(
@@ -496,16 +536,36 @@
         cost_estimate=cost(8 * rows * width),
         name="join",
     )(*pieces)
-    grad_keys, grad_values = pl.pallas_call(
+    in_hbm = pl.BlockSpec(memory_space=pltpu.HBM)
+    gradients = pl.pallas_call(
         functools.partial(add_kernel, plan),
         out_shape=[shape((rows, width), low)] * 2,
-        in_specs=[scalars] * 2 + [whole] * (members + len(border_terms)),
-        out_specs=[pl.BlockSpec(memory_space=pltpu.HBM)] * 2,
+        in_specs=[scalars] * 2 + [whole] * (3 * members),
+        out_specs=[in_hbm] * 2,
         scratch_shapes=[pltpu.VMEM((2, rows, width), low), pltpu.SemaphoreType.DMA((2 * plan.device_tiles,))],
         compiler_params=params,
-        cost_estimate=cost(10 * rows * width),
+        cost_estimate=cost(20 * rows * width),
         name="add",
-    )(lists, tile_counts, *pieces, *border_terms)
+    )(lists, tile_counts, *pieces, *everyone(nears[0], fars[0]))
+    if chunks > 1:
+        places = 2 * plan.device_tiles * members
+        written = [pltpu.with_memory_space_constraint(x, pltpu.HBM) for x in (attended, gradients[0])]
+        late = hold("hold_last", written, nears[1], fars[1])
+        gradients = pl.pallas_call(
+            functools.partial(patch_kernel, plan),
+            out_shape=[shape((rows, width), low)] * 2,
+            in_specs=[scalars] * 2 + [whole] * (3 * members) + [in_hbm] * 2,
+            out_specs=[in_hbm] * 2,
+            scratch_shapes=[
+                pltpu.VMEM((places, TILE, plan.chunk_pairs[1] * PAIR), low),
+                pltpu.SemaphoreType.DMA((places,)),
+            ],
+            input_output_aliases={2 + 3 * members: 0, 3 + 3 * members: 1},
+            compiler_params=params,
+            cost_estimate=cost(4 * rows * width),
+            name="patch",
+        )(lists, tile_counts, *pieces, *everyone(*late), *gradients)
+    grad_keys, grad_values = gradients
     return attended, grad_queries, grad_keys, grad_values
 
 

time: 51.8 us -> 51.7 us (level)
  Pallas kernels: 13.2 us -> 14.7 us
  waiting for transfers between devices: 12.7 us -> 11.3 us
    ppermute x2, waiting for transfers between devices: 8.47 us -> 5.53 us  [per_device(): nears.append(lax.ppermute(parts[0], axes, plan.frame_perm(0)))]
    pallas_call x0 -> x1, Pallas kernels: none -> 1.58 us  [per_device(): pl.pallas_call(functools.partial(patch_kernel, plan), out_shape=[shape((r...]
    ppermute x5, waiting for transfers between devices: 0.19 us -> 1.68 us  [home(): return lax.ppermute(sent, axes, plan.member_perm(members - r))]
  transfers between devices with their start and end apart: 17 -> 17, of which waited for: 6 -> 8; matrix products, arithmetic and copies ran while one was open for 0% -> 0% of each run, Pallas kernels for 21% -> 25%
where the time goes in v2:
time: 51.7 us; the launch traced here: 51.5 us
  starting transfers between devices  22.4 us (43%)
  Pallas kernels  14.7 us (28%)
  waiting for transfers between devices  11.3 us (22%)
  local copies, waits for them, and re-layouts  2.28 us (4%)
  between operations  0.84 us (2%)
    ppermute x5, starting transfers between devices, home(): return lax.ppermute(sent, axes, plan.member_perm(members - r))  8.79 us
    pallas_call x2, Pallas kernels, per_device(): pl.pallas_call(functools.partial(attend_kernel, plan, g), out_shape=[shap...  8.19 us
    ppermute x4, starting transfers between devices, per_device(): lax.ppermute(x, axes, plan.frame_perm(i))  6.66 us
    ppermute x2, waiting for transfers between devices, per_device(): nears.append(lax.ppermute(parts[0], axes, plan.frame_perm(0)))  5.53 us
    ppermute x2, starting transfers between devices, per_device(): fars.append(lax.ppermute(parts[1], axes, plan.frame_perm(1)))  4.11 us
    ppermute x4, waiting for transfers between devices, per_device(): lax.ppermute(x, axes, plan.frame_perm(i))  3.02 us
    unnamed x14, local copies, waits for them, and re-layouts  2.28 us
    pallas_call x1, Pallas kernels, per_device(): pl.pallas_call(functools.partial(add_kernel, plan), out_shape=[shape((row...  1.97 us
  transfers between devices with their start and end apart: 17, of which 8 were waited for; matrix products, arithmetic and copies ran while one was open for 0% of the time, Pallas kernels for 25%

profile of v2, /device:TPU:21, one launch (start us, length us, event | category | flops | bytes accessed | tf_op | source)
XLA Modules:
  0.0 51.5 jit_solution(14854592834802926304)
XLA Ops:
  0.6 0.0 copy-start
  0.6 0.0 copy-start.1
  0.7 0.7 %collective-permute-start = (bf16[128,3072]{1,0:T(8,128)(2,1)}, bf16[128,3072]{1,0:T(8,128)(2,1)S(1)}, u32[]{:S(2)}, u32[]{:S(2)}) collective-permute-start(bf16[128,3072]{1,0:T(8,128)(2,1)} %refs_1_.9), channel_id=1, source_target_pairs={{0,4},{4,0},{8,12},{12,8},{1,5},{5,1},{9,13},{13,9},{2,6},{6,2},{1... | collective-permute-start | bytes 2359304 | tf_op jit(solution)/shard_map/ppermute | solution.py:437
  1.4 0.1 collective-permute-start.1
  1.5 1.1 %copy-done.2 = bf16[128,3072]{1,0:T(8,128)(2,1)S(1)} copy-done((bf16[128,3072]{1,0:T(8,128)(2,1)S(1)}, bf16[128,3072]{1,0:T(8,128)(2,1)}, u32[]{:S(2)}) %copy-start.2) | copy-done | bytes 786456
  2.6 1.1 %copy-done.4 = bf16[128,3072]{1,0:T(8,128)(2,1)S(1)} copy-done((bf16[128,3072]{1,0:T(8,128)(2,1)S(1)}, bf16[128,3072]{1,0:T(8,128)(2,1)}, u32[]{:S(2)}) %copy-start.4) | copy-done | bytes 786456
  3.7 0.1 split_qg.1
  3.8 0.5 collective-permute-start.2
  4.3 0.1 collective-permute-start.3
  4.4 0.0 collective-permute-done.refs_2_.refs_4_
  4.4 0.3 collective-permute-done.1.refs_3_.refs_5_
  4.6 0.0 copy-done.1
  4.7 0.7 %pick_0.1 = (bf16[2,1,64,768]{3,2,1,0:T(8,128)(2,1)S(1)}, bf16[2,1,64,768]{3,2,1,0:T(8,128)(2,1)S(1)}) custom-call(s32[3,32]{1,0:T(4,128)S(1)} %bitcast.1, s32[32]{0:T(128)S(1)} %copy-done.6, bf16[128,3072]{1,0:T(8,128)(2,1)S(1)} %copy-done, bf16[128,3072]{1,0:T(8,128)(2,1)S(1)} %copy-done.1, bf16[128,3072]{1,0:T(8,128)(2,1)S(1)} %collective-permute-done.refs_2_.refs_4_, ...), custom_call_target="tpu_custom_call" | custom-call | bytes 786432 | tf_op jit(solution)/shard_map/pick_0/pallas_call | solution.py:475
  5.4 0.3 collective-permute-start.4
  5.7 4.3 %collective-permute-start.7 = (bf16[2,1,64,768]{3,2,1,0:T(8,128)(2,1)S(1)}, bf16[2,1,64,768]{3,2,1,0:T(8,128)(2,1)S(1)}, u32[]{:S(2)}, u32[]{:S(2)}) collective-permute-start(bf16[2,1,64,768]{3,2,1,0:T(8,128)(2,1)S(1)} %get-tuple-element.33), channel_id=1, source_target_pairs={{8,1},{12,5},{1,8},{5,12},{9,2},{13,6},{2,9},{6,13},{10,3},{14,7},... | collective-permute-start | bytes 589832 | tf_op jit(solution)/shard_map/ppermute | solution.py:487
  10.0 0.7 %pick_1.1 = (bf16[2,1,64,768]{3,2,1,0:T(8,128)(2,1)S(1)}, bf16[2,1,64,768]{3,2,1,0:T(8,128)(2,1)S(1)}) custom-call(s32[3,32]{1,0:T(4,128)S(1)} %bitcast.2, s32[32]{0:T(128)S(1)} %copy-done.6, bf16[128,3072]{1,0:T(8,128)(2,1)S(1)} %copy-done, bf16[128,3072]{1,0:T(8,128)(2,1)S(1)} %copy-done.1, bf16[128,3072]{1,0:T(8,128)(2,1)S(1)} %collective-permute-done.refs_2_.refs_4_, ...), custom_call_target="tpu_custom_call" | custom-call | bytes 786432 | tf_op jit(solution)/shard_map/pick_1/pallas_call | solution.py:475
  10.8 2.0 %collective-permute-start.6 = (bf16[2,1,64,768]{3,2,1,0:T(8,128)(2,1)S(1)}, bf16[2,1,64,768]{3,2,1,0:T(8,128)(2,1)S(1)}, u32[]{:S(2)}, u32[]{:S(2)}) collective-permute-start(bf16[2,1,64,768]{3,2,1,0:T(8,128)(2,1)S(1)} %get-tuple-element.32), channel_id=1, source_target_pairs={{8,1},{12,5},{1,8},{5,12},{9,2},{13,6},{2,9},{6,13},{10,3},{14,7},... | collective-permute-start | bytes 589832 | tf_op jit(solution)/shard_map/ppermute | solution.py:487
  12.8 3.0 %collective-permute-done.4.refs_0_.refs_8_ = bf16[2,1,64,768]{3,2,1,0:T(8,128)(2,1)S(1)} collective-permute-done((bf16[2,1,64,768]{3,2,1,0:T(8,128)(2,1)S(1)}, bf16[2,1,64,768]{3,2,1,0:T(8,128)(2,1)S(1)}, u32[]{:S(2)}, u32[]{:S(2)}) %collective-permute-start.4) | collective-permute-done | bytes 196640 | tf_op jit(solution)/shard_map/ppermute | solution.py:487
  15.8 0.1 collective-permute-start.5
  15.9 0.0 collective-permute-done.2.refs_6_
  15.9 0.0 collective-permute-done.3.refs_7_
  15.9 0.0 collective-permute-done.7.refs_9_
  15.9 4.1 %attend_0.1 = (bf16[4,128,768]{2,1,0:T(8,128)(2,1)S(1)}, bf16[4,128,768]{2,1,0:T(8,128)(2,1)S(1)}, bf16[2,1,64,768]{3,2,1,0:T(8,128)(2,1)S(1)}, bf16[2,1,64,768]{3,2,1,0:T(8,128)(2,1)S(1)}) custom-call(s32[3,32]{1,0:T(4,128)S(1)} %bitcast.3, s32[32]{0:T(128)S(1)} %copy-done.6, bf16[128,3072]{1,0:T(8,128)(2,1)S(1)} %copy-done.3, ...), custom_call_target="tpu_custom_call" | custom-call | flops 905969664 | bytes 3145728 | tf_op jit(solution)/shard_map/attend_0/pallas_call | solution.py:498
  20.0 1.5 %collective-permute-start.8 = (bf16[2,1,64,768]{3,2,1,0:T(8,128)(2,1)S(1)}, bf16[2,1,64,768]{3,2,1,0:T(8,128)(2,1)S(1)}, u32[]{:S(2)}, u32[]{:S(2)}) collective-permute-start(bf16[2,1,64,768]{3,2,1,0:T(8,128)(2,1)S(1)} %get-tuple-element.37), channel_id=1, source_target_pairs={{0,8},{4,12},{8,0},{12,4},{1,9},{5,13},{9,1},{13,5},{2,10},{6,14},... | collective-permute-start | bytes 589832 | tf_op jit(solution)/shard_map/ppermute | solution.py:522
  21.5 1.9 %collective-permute-start.9 = (bf16[2,1,64,768]{3,2,1,0:T(8,128)(2,1)S(1)}, bf16[2,1,64,768]{3,2,1,0:T(8,128)(2,1)S(1)}, u32[]{:S(2)}, u32[]{:S(2)}) collective-permute-start(bf16[2,1,64,768]{3,2,1,0:T(8,128)(2,1)S(1)} %get-tuple-element.38), channel_id=1, source_target_pairs={{8,1},{12,5},{1,8},{5,12},{9,2},{13,6},{2,9},{6,13},{10,3},{14,7},... | collective-permute-start | bytes 589832 | tf_op jit(solution)/shard_map/ppermute | solution.py:523
  23.4 0.0 collective-permute-done.6.refs_9_
  23.4 0.0 collective-permute-done.5.refs_8_
  23.4 4.1 %attend_1.1 = (bf16[4,128,1536]{2,1,0:T(8,128)(2,1)S(1)}, bf16[4,128,1536]{2,1,0:T(8,128)(2,1)S(1)}, bf16[2,1,64,768]{3,2,1,0:T(8,128)(2,1)S(1)}, bf16[2,1,64,768]{3,2,1,0:T(8,128)(2,1)S(1)}) custom-call(s32[3,32]{1,0:T(4,128)S(1)} %bitcast.4, s32[32]{0:T(128)S(1)} %copy-done.6, bf16[128,3072]{1,0:T(8,128)(2,1)S(1)} %copy-done.3, ...), custom_call_target="tpu_custom_call" | custom-call | flops 905969664 | bytes 3145728 | tf_op jit(solution)/shard_map/attend_1/pallas_call | solution.py:498
  27.6 0.6 %collective-permute-done.8.refs_0_.refs_2_ = bf16[2,1,64,768]{3,2,1,0:T(8,128)(2,1)S(1)} collective-permute-done((bf16[2,1,64,768]{3,2,1,0:T(8,128)(2,1)S(1)}, bf16[2,1,64,768]{3,2,1,0:T(8,128)(2,1)S(1)}, u32[]{:S(2)}, u32[]{:S(2)}) %collective-permute-start.8) | collective-permute-done | bytes 196640 | tf_op jit(solution)/shard_map/ppermute | solution.py:522
  28.1 0.8 %collective-permute-done.9.refs_1_.refs_3_ = bf16[2,1,64,768]{3,2,1,0:T(8,128)(2,1)S(1)} collective-permute-done((bf16[2,1,64,768]{3,2,1,0:T(8,128)(2,1)S(1)}, bf16[2,1,64,768]{3,2,1,0:T(8,128)(2,1)S(1)}, u32[]{:S(2)}, u32[]{:S(2)}) %collective-permute-start.9) | collective-permute-done | bytes 196640 | tf_op jit(solution)/shard_map/ppermute | solution.py:523
  28.9 0.1 hold_far_1.1
  29.0 7.3 %collective-permute-start.10 = (bf16[4,128,1536]{2,1,0:T(8,128)(2,1)S(1)}, bf16[4,128,1536]{2,1,0:T(8,128)(2,1)S(1)}, u32[]{:S(2)}, u32[]{:S(2)}) collective-permute-start(bf16[4,128,1536]{2,1,0:T(8,128)(2,1)S(1)} %get-tuple-element.41), channel_id=1, source_target_pairs={{0,4},{4,0},{8,12},{12,8},{1,5},{5,1},{9,13},{13,9},{2,6},{6,2},{1... | collective-permute-start | bytes 4718600 | tf_op jit(solution)/shard_map/ppermute | solution.py:491
  36.3 0.1 collective-permute-start.11
  36.4 0.4 collective-permute-start.12
  36.8 0.0 collective-permute-start.13
  36.8 2.2 %collective-permute-start.14 = (bf16[2,1,64,768]{3,2,1,0:T(8,128)(2,1)S(1)}, bf16[2,1,64,768]{3,2,1,0:T(8,128)(2,1)S(1)}, u32[]{:S(2)}, u32[]{:S(2)}) collective-permute-start(bf16[2,1,64,768]{3,2,1,0:T(8,128)(2,1)S(1)} %get-tuple-element.46), channel_id=1, source_target_pairs={{8,1},{12,5},{1,8},{5,12},{9,2},{13,6},{2,9},{6,13},{10,3},{14,7},... | collective-permute-start | bytes 589832 | tf_op jit(solution)/shard_map/ppermute | solution.py:523
  39.0 0.3 collective-permute-done.10.refs_1_
  39.3 1.2 %join.1 = (bf16[128,3072]{1,0:T(8,128)(2,1)}, bf16[128,3072]{1,0:T(8,128)(2,1)}) custom-call(bf16[4,128,1536]{2,1,0:T(8,128)(2,1)S(1)} %get-tuple-element.36.refs_0_, bf16[4,128,1536]{2,1,0:T(8,128)(2,1)S(1)} %collective-permute-done.10.refs_1_), custom_call_target="tpu_custom_call" | custom-call | bytes 3145728 | tf_op jit(solution)/shard_map/join/pallas_call | solution.py:529
  40.6 0.0 collective-permute-done.11.refs_4_
  40.6 0.0 collective-permute-done.12.refs_5_
  40.6 2.0 %add.1 = (bf16[128,3072]{1,0:T(8,128)(2,1)}, bf16[128,3072]{1,0:T(8,128)(2,1)}) custom-call(s32[3,32]{1,0:T(4,128)S(1)} %bitcast.5, s32[32]{0:T(128)S(1)} %copy-done.6, bf16[4,128,1536]{2,1,0:T(8,128)(2,1)S(1)} %get-tuple-element.36.refs_0_, bf16[4,128,1536]{2,1,0:T(8,128)(2,1)S(1)} %collective-permute-done.10.refs_1_, ...), custom_call_target="tpu_custom_call" | custom-call | bytes 7864320 | tf_op jit(solution)/shard_map/add/pallas_call | solution.py:540
  42.6 5.0 %collective-permute-done.13.refs_2_ = bf16[2,1,64,768]{3,2,1,0:T(8,128)(2,1)S(1)} collective-permute-done((bf16[2,1,64,768]{3,2,1,0:T(8,128)(2,1)S(1)}, bf16[2,1,64,768]{3,2,1,0:T(8,128)(2,1)S(1)}, u32[]{:S(2)}, u32[]{:S(2)}) %collective-permute-start.13) | collective-permute-done | bytes 196640 | tf_op jit(solution)/shard_map/ppermute | solution.py:522
  47.5 0.0 collective-permute-done.14.refs_3_
  47.5 0.9 %collective-permute-start.15 = (bf16[2,1,64,768]{3,2,1,0:T(8,128)(2,1)S(1)}, bf16[2,1,64,768]{3,2,1,0:T(8,128)(2,1)S(1)}, u32[]{:S(2)}, u32[]{:S(2)}) collective-permute-start(bf16[2,1,64,768]{3,2,1,0:T(8,128)(2,1)S(1)} %get-tuple-element.47.refs_2_), channel_id=1, source_target_pairs={{0,4},{4,0},{8,12},{12,8},{1,5},{5,1},{9,13},{13,9},{2,6},{6,2},{1... | collective-permute-start | bytes 589832 | tf_op jit(solution)/shard_map/ppermute | solution.py:491
  48.5 0.1 collective-permute-start.16
  48.5 1.0 %collective-permute-done.15.refs_4_ = bf16[2,1,64,768]{3,2,1,0:T(8,128)(2,1)S(1)} collective-permute-done((bf16[2,1,64,768]{3,2,1,0:T(8,128)(2,1)S(1)}, bf16[2,1,64,768]{3,2,1,0:T(8,128)(2,1)S(1)}, u32[]{:S(2)}, u32[]{:S(2)}) %collective-permute-start.15) | collective-permute-done | bytes 196640 | tf_op jit(solution)/shard_map/ppermute | solution.py:491
  49.5 0.4 collective-permute-done.16.refs_5_
  49.9 1.6 %patch.1 = (bf16[128,3072]{1,0:T(8,128)(2,1)}, bf16[128,3072]{1,0:T(8,128)(2,1)}) custom-call(s32[3,32]{1,0:T(4,128)S(1)} %bitcast.6, s32[32]{0:T(128)S(1)} %copy-done.6, bf16[4,128,1536]{2,1,0:T(8,128)(2,1)S(1)} %get-tuple-element.36.refs_0_, ...), custom_call_target="tpu_custom_call", output_to_operand_aliasing={{0}: (8, {}), {1}: (9, {})} | custom-call | bytes 1572864 | tf_op jit(solution)/shard_map/patch/pallas_call | solution.py:554
  (11 shorter events, 0.1 us)
Async XLA Ops:
  0.6 4.0 %copy-start = (bf16[128,3072]{1,0:T(8,128)(2,1)S(1)}, bf16[128,3072]{1,0:T(8,128)(2,1)}, u32[]{:S(2)}) copy-start(bf16[128,3072]{1,0:T(8,128)(2,1)} %refs_1_.9) | copy-start | bytes 2359300
  0.6 4.0 %copy-start.1 = (bf16[128,3072]{1,0:T(8,128)(2,1)S(1)}, bf16[128,3072]{1,0:T(8,128)(2,1)}, u32[]{:S(2)}) copy-start(bf16[128,3072]{1,0:T(8,128)(2,1)} %refs_2_.3) | copy-start | bytes 2359300
  0.7 3.7 %collective-permute-start = (bf16[128,3072]{1,0:T(8,128)(2,1)}, bf16[128,3072]{1,0:T(8,128)(2,1)S(1)}, u32[]{:S(2)}, u32[]{:S(2)}) collective-permute-start(bf16[128,3072]{1,0:T(8,128)(2,1)} %refs_1_.9), channel_id=1, source_target_pairs={{0,4},{4,0},{8,12},{12,8},{1,5},{5,1},{9,13},{13,9},{2,6},{6,2},{1... | collective-permute-start | bytes 2359304 | tf_op jit(solution)/shard_map/ppermute | solution.py:437
  1.4 3.2 %collective-permute-start.1 = (bf16[128,3072]{1,0:T(8,128)(2,1)}, bf16[128,3072]{1,0:T(8,128)(2,1)S(1)}, u32[]{:S(2)}, u32[]{:S(2)}) collective-permute-start(bf16[128,3072]{1,0:T(8,128)(2,1)} %refs_2_.3), channel_id=1, source_target_pairs={{0,4},{4,0},{8,12},{12,8},{1,5},{5,1},{9,13},{13,9},{2,6},{6,2},{1... | collective-permute-start | bytes 2359304 | tf_op jit(solution)/shard_map/ppermute | solution.py:437
  1.5 1.1 %copy-start.2 = (bf16[128,3072]{1,0:T(8,128)(2,1)S(1)}, bf16[128,3072]{1,0:T(8,128)(2,1)}, u32[]{:S(2)}) copy-start(bf16[128,3072]{1,0:T(8,128)(2,1)} %refs_0_.9) | copy-start | bytes 2359300
  2.6 1.1 %copy-start.4 = (bf16[128,3072]{1,0:T(8,128)(2,1)S(1)}, bf16[128,3072]{1,0:T(8,128)(2,1)}, u32[]{:S(2)}) copy-start(bf16[128,3072]{1,0:T(8,128)(2,1)} %refs_3_.3) | copy-start | bytes 2359300
  3.7 0.9 %copy-start.5 = (s32[32,3]{0,1:T(4,128)S(1)}, s32[32,3]{0,1:T(4,128)}, u32[]{:S(2)}) copy-start(s32[32,3]{0,1:T(4,128)} %param.10) | copy-start | bytes 1156
  3.7 0.9 %copy-start.6 = (s32[32]{0:T(128)S(1)}, s32[32]{0:T(128)}, u32[]{:S(2)}) copy-start(s32[32]{0:T(128)} %counts_ref.11) | copy-start | bytes 388
  3.8 12.1 %collective-permute-start.2 = (bf16[128,1536]{1,0:T(8,128)(2,1)S(1)}, bf16[128,1536]{1,0:T(8,128)(2,1)S(1)}, u32[]{:S(2)}, u32[]{:S(2)}) collective-permute-start(bf16[128,1536]{1,0:T(8,128)(2,1)S(1)} %get-tuple-element.28), channel_id=1, source_target_pairs={{0,4},{4,0},{8,12},{12,8},{1,5},{5,1},{9,13},{13,9},{2,6},{6,2},{1... | collective-permute-start | bytes 1179656 | tf_op jit(solution)/shard_map/ppermute | solution.py:453
  4.3 11.6 %collective-permute-start.3 = (bf16[128,1536]{1,0:T(8,128)(2,1)S(1)}, bf16[128,1536]{1,0:T(8,128)(2,1)S(1)}, u32[]{:S(2)}, u32[]{:S(2)}) collective-permute-start(bf16[128,1536]{1,0:T(8,128)(2,1)S(1)} %get-tuple-element.29), channel_id=1, source_target_pairs={{0,4},{4,0},{8,12},{12,8},{1,5},{5,1},{9,13},{13,9},{2,6},{6,2},{1... | collective-permute-start | bytes 1179656 | tf_op jit(solution)/shard_map/ppermute | solution.py:453
  5.4 10.4 %collective-permute-start.4 = (bf16[2,1,64,768]{3,2,1,0:T(8,128)(2,1)S(1)}, bf16[2,1,64,768]{3,2,1,0:T(8,128)(2,1)S(1)}, u32[]{:S(2)}, u32[]{:S(2)}) collective-permute-start(bf16[2,1,64,768]{3,2,1,0:T(8,128)(2,1)S(1)} %get-tuple-element.30), channel_id=1, source_target_pairs={{0,8},{4,12},{8,0},{12,4},{1,9},{5,13},{9,1},{13,5},{2,10},{6,14},... | collective-permute-start | bytes 589832 | tf_op jit(solution)/shard_map/ppermute | solution.py:487
  5.7 10.2 %copy-start.3 = (bf16[128,3072]{1,0:T(8,128)(2,1)S(1)}, bf16[128,3072]{1,0:T(8,128)(2,1)}, u32[]{:S(2)}) copy-start(bf16[128,3072]{1,0:T(8,128)(2,1)} %refs_0_.9) | copy-start | bytes 2359300
  5.7 10.2 %collective-permute-start.7 = (bf16[2,1,64,768]{3,2,1,0:T(8,128)(2,1)S(1)}, bf16[2,1,64,768]{3,2,1,0:T(8,128)(2,1)S(1)}, u32[]{:S(2)}, u32[]{:S(2)}) collective-permute-start(bf16[2,1,64,768]{3,2,1,0:T(8,128)(2,1)S(1)} %get-tuple-element.33), channel_id=1, source_target_pairs={{8,1},{12,5},{1,8},{5,12},{9,2},{13,6},{2,9},{6,13},{10,3},{14,7},... | collective-permute-start | bytes 589832 | tf_op jit(solution)/shard_map/ppermute | solution.py:487
  10.8 12.7 %collective-permute-start.6 = (bf16[2,1,64,768]{3,2,1,0:T(8,128)(2,1)S(1)}, bf16[2,1,64,768]{3,2,1,0:T(8,128)(2,1)S(1)}, u32[]{:S(2)}, u32[]{:S(2)}) collective-permute-start(bf16[2,1,64,768]{3,2,1,0:T(8,128)(2,1)S(1)} %get-tuple-element.32), channel_id=1, source_target_pairs={{8,1},{12,5},{1,8},{5,12},{9,2},{13,6},{2,9},{6,13},{10,3},{14,7},... | collective-permute-start | bytes 589832 | tf_op jit(solution)/shard_map/ppermute | solution.py:487
  15.8 7.6 %collective-permute-start.5 = (bf16[2,1,64,768]{3,2,1,0:T(8,128)(2,1)S(1)}, bf16[2,1,64,768]{3,2,1,0:T(8,128)(2,1)S(1)}, u32[]{:S(2)}, u32[]{:S(2)}) collective-permute-start(bf16[2,1,64,768]{3,2,1,0:T(8,128)(2,1)S(1)} %hold_near_1.1), channel_id=1, source_target_pairs={{0,8},{4,12},{8,0},{12,4},{1,9},{5,13},{9,1},{13,5},{2,10},{6,14},... | collective-permute-start | bytes 589832 | tf_op jit(solution)/shard_map/ppermute | solution.py:487
  20.0 8.1 %collective-permute-start.8 = (bf16[2,1,64,768]{3,2,1,0:T(8,128)(2,1)S(1)}, bf16[2,1,64,768]{3,2,1,0:T(8,128)(2,1)S(1)}, u32[]{:S(2)}, u32[]{:S(2)}) collective-permute-start(bf16[2,1,64,768]{3,2,1,0:T(8,128)(2,1)S(1)} %get-tuple-element.37), channel_id=1, source_target_pairs={{0,8},{4,12},{8,0},{12,4},{1,9},{5,13},{9,1},{13,5},{2,10},{6,14},... | collective-permute-start | bytes 589832 | tf_op jit(solution)/shard_map/ppermute | solution.py:522
  21.5 7.4 %collective-permute-start.9 = (bf16[2,1,64,768]{3,2,1,0:T(8,128)(2,1)S(1)}, bf16[2,1,64,768]{3,2,1,0:T(8,128)(2,1)S(1)}, u32[]{:S(2)}, u32[]{:S(2)}) collective-permute-start(bf16[2,1,64,768]{3,2,1,0:T(8,128)(2,1)S(1)} %get-tuple-element.38), channel_id=1, source_target_pairs={{8,1},{12,5},{1,8},{5,12},{9,2},{13,6},{2,9},{6,13},{10,3},{14,7},... | collective-permute-start | bytes 589832 | tf_op jit(solution)/shard_map/ppermute | solution.py:523
  29.0 10.3 %collective-permute-start.10 = (bf16[4,128,1536]{2,1,0:T(8,128)(2,1)S(1)}, bf16[4,128,1536]{2,1,0:T(8,128)(2,1)S(1)}, u32[]{:S(2)}, u32[]{:S(2)}) collective-permute-start(bf16[4,128,1536]{2,1,0:T(8,128)(2,1)S(1)} %get-tuple-element.41), channel_id=1, source_target_pairs={{0,4},{4,0},{8,12},{12,8},{1,5},{5,1},{9,13},{13,9},{2,6},{6,2},{1... | collective-permute-start | bytes 4718600 | tf_op jit(solution)/shard_map/ppermute | solution.py:491
  36.3 4.3 %collective-permute-start.11 = (bf16[2,1,64,768]{3,2,1,0:T(8,128)(2,1)S(1)}, bf16[2,1,64,768]{3,2,1,0:T(8,128)(2,1)S(1)}, u32[]{:S(2)}, u32[]{:S(2)}) collective-permute-start(bf16[2,1,64,768]{3,2,1,0:T(8,128)(2,1)S(1)} %collective-permute-done.8.refs_0_.refs_2_), channel_id=1, source_target_pairs={{0,4},{4,0},{8,12},{12,8},{1,5},{5,1},{9,13},{13,9},{2,6},{6,2},{1... | collective-permute-start | bytes 589832 | tf_op jit(solution)/shard_map/ppermute | solution.py:491
  36.4 4.2 %collective-permute-start.12 = (bf16[2,1,64,768]{3,2,1,0:T(8,128)(2,1)S(1)}, bf16[2,1,64,768]{3,2,1,0:T(8,128)(2,1)S(1)}, u32[]{:S(2)}, u32[]{:S(2)}) collective-permute-start(bf16[2,1,64,768]{3,2,1,0:T(8,128)(2,1)S(1)} %collective-permute-done.9.refs_1_.refs_3_), channel_id=1, source_target_pairs={{0,4},{4,0},{8,12},{12,8},{1,5},{5,1},{9,13},{13,9},{2,6},{6,2},{1... | collective-permute-start | bytes 589832 | tf_op jit(solution)/shard_map/ppermute | solution.py:491
  36.8 10.7 %collective-permute-start.13 = (bf16[2,1,64,768]{3,2,1,0:T(8,128)(2,1)S(1)}, bf16[2,1,64,768]{3,2,1,0:T(8,128)(2,1)S(1)}, u32[]{:S(2)}, u32[]{:S(2)}) collective-permute-start(bf16[2,1,64,768]{3,2,1,0:T(8,128)(2,1)S(1)} %get-tuple-element.45), channel_id=1, source_target_pairs={{0,8},{4,12},{8,0},{12,4},{1,9},{5,13},{9,1},{13,5},{2,10},{6,14},... | collective-permute-start | bytes 589832 | tf_op jit(solution)/shard_map/ppermute | solution.py:522
  36.8 10.7 %collective-permute-start.14 = (bf16[2,1,64,768]{3,2,1,0:T(8,128)(2,1)S(1)}, bf16[2,1,64,768]{3,2,1,0:T(8,128)(2,1)S(1)}, u32[]{:S(2)}, u32[]{:S(2)}) collective-permute-start(bf16[2,1,64,768]{3,2,1,0:T(8,128)(2,1)S(1)} %get-tuple-element.46), channel_id=1, source_target_pairs={{8,1},{12,5},{1,8},{5,12},{9,2},{13,6},{2,9},{6,13},{10,3},{14,7},... | collective-permute-start | bytes 589832 | tf_op jit(solution)/shard_map/ppermute | solution.py:523
  47.5 2.0 %collective-permute-start.15 = (bf16[2,1,64,768]{3,2,1,0:T(8,128)(2,1)S(1)}, bf16[2,1,64,768]{3,2,1,0:T(8,128)(2,1)S(1)}, u32[]{:S(2)}, u32[]{:S(2)}) collective-permute-start(bf16[2,1,64,768]{3,2,1,0:T(8,128)(2,1)S(1)} %get-tuple-element.47.refs_2_), channel_id=1, source_target_pairs={{0,4},{4,0},{8,12},{12,8},{1,5},{5,1},{9,13},{13,9},{2,6},{6,2},{1... | collective-permute-start | bytes 589832 | tf_op jit(solution)/shard_map/ppermute | solution.py:491
  48.5 1.4 %collective-permute-start.16 = (bf16[2,1,64,768]{3,2,1,0:T(8,128)(2,1)S(1)}, bf16[2,1,64,768]{3,2,1,0:T(8,128)(2,1)S(1)}, u32[]{:S(2)}, u32[]{:S(2)}) collective-permute-start(bf16[2,1,64,768]{3,2,1,0:T(8,128)(2,1)S(1)} %get-tuple-element.48.refs_3_), channel_id=1, source_target_pairs={{0,4},{4,0},{8,12},{12,8},{1,5},{5,1},{9,13},{13,9},{2,6},{6,2},{1... | collective-permute-start | bytes 589832 | tf_op jit(solution)/shard_map/ppermute | solution.py:491
